TPU v7x, 512 devices: a whole 4x4x16 slice. The times are simulated.
512 devices in a mesh: pos: 128 (over y, z, core), mode: 4 (over x).
Axes of the slice: x: 4, y: 4, z: 16, core: 2. Of those that a mesh axis runs over, the one named last changes fastest.
Arguments:
- tiles: float32 [128, 2, 2, 128, 128], P('pos'), may hold values from -5 to 5
- probe: float32 [4, 2, 128, 128], P('mode'), may hold values from -5 to 5
- fresnel_phase: float32 [128, 128], replicated, may hold values from -3.140625 to 3.140625
- offsets: int32 [512, 2], P('pos'), may hold values from 0 to 3968, as said below
- measured: float32 [512, 128, 128], P('pos'), may hold values from 0 to 8
Outputs:
- object_grad: float32 [128, 2, 2, 128, 128], P('pos', None, None, 'mode')
- probe_grad: float32 [4, 2, 128, 128], P('mode')
Inputs may be any that keep to these rules, and one draw needn't show every extreme that they name: `offsets`: position q belongs to tile q // 4: its top-left corner lies in that tile, and its whole window lies inside the object.
All inputs are finite; a program needn't handle non-finite values.
Results may differ from a plain program's by a relative error of at most 0.0003.
Values sent between devices are 32-bit elements; how exact they have to be, the bound alone decides.
A program may use at most 64 MiB of HBM per device.

v0:
```python
import math

import jax
import jax.numpy as jnp
from jax import lax
from jax.sharding import PartitionSpec as P

SLICES = 2
TILE_COLS = 4


def shifted(value, axis, steps):
    count = lax.axis_size(axis)
    initial, last = (max(0, -steps), min(count, count - steps))
    return lax.ppermute(value, axis, [(source, source + steps) for source in range(initial, last)])


def tables(size):
    index = jnp.arange(size)
    angle = (index[:, None] * index[None, :] % size).astype(jnp.float32) * (2.0 * math.pi / size)
    factor = 1.0 / math.sqrt(size)
    return (jnp.cos(angle) * factor, jnp.sin(angle) * factor)


def transform(real, imag, cosines, sines, sign):
    highest = lax.Precision.HIGHEST
    signed = sines * sign

    def left_side(table, data):
        return jnp.einsum("jk,...kl->...jl", table, data, precision=highest)

    def right_side(data, table):
        return jnp.einsum("...jk,kl->...jl", data, table, precision=highest)

    first_re = left_side(cosines, real) - left_side(signed, imag)
    first_im = left_side(cosines, imag) + left_side(signed, real)
    out_re = right_side(first_re, cosines) - right_side(first_im, signed)
    out_im = right_side(first_im, cosines) + right_side(first_re, signed)
    return (out_re, out_im)


def complex_mul(a_re, a_im, b_re, b_im):
    return (a_re * b_re - a_im * b_im, a_re * b_im + a_im * b_re)


def conj_mul(a_re, a_im, b_re, b_im):
    return (a_re * b_re + a_im * b_im, a_re * b_im - a_im * b_re)


def propagate(
    probe_re, probe_im, front_re, front_im, back_re, back_im, target, summing, fresnel_phase
):
    size = fresnel_phase.shape[-1]
    cosines, sines = tables(size)
    kernel_re = jnp.cos(fresnel_phase)
    kernel_im = jnp.sin(fresnel_phase)
    exit_re, exit_im = complex_mul(probe_re, probe_im, front_re, front_im)
    spec_re, spec_im = transform(exit_re, exit_im, cosines, sines, -1.0)
    spec_re, spec_im = complex_mul(spec_re, spec_im, kernel_re, kernel_im)
    wave_re, wave_im = transform(spec_re, spec_im, cosines, sines, 1.0)
    last_re, last_im = complex_mul(wave_re, wave_im, back_re, back_im)
    far_re, far_im = transform(last_re, last_im, cosines, sines, -1.0)
    intensity = summing(far_re * far_re + far_im * far_im)
    resid = intensity - target
    chi_re, chi_im = (resid * far_re, resid * far_im)
    grad_re, grad_im = transform(chi_re, chi_im, cosines, sines, 1.0)
    back_obj_re, back_obj_im = conj_mul(wave_re, wave_im, grad_re, grad_im)
    inner_re, inner_im = conj_mul(back_re, back_im, grad_re, grad_im)
    spec_re, spec_im = transform(inner_re, inner_im, cosines, sines, -1.0)
    spec_re, spec_im = conj_mul(kernel_re, kernel_im, spec_re, spec_im)
    first_re, first_im = transform(spec_re, spec_im, cosines, sines, 1.0)
    front_obj_re, front_obj_im = conj_mul(probe_re, probe_im, first_re, first_im)
    probe_re_term, probe_im_term = conj_mul(front_re, front_im, first_re, first_im)
    return (front_obj_re, front_obj_im, back_obj_re, back_obj_im, probe_re_term, probe_im_term)


def body(tiles, probe, fresnel_phase, offsets, measured):
    own = tiles[0]
    size = probe.shape[-1]
    edge = own.shape[-1]
    count = offsets.shape[0]
    right = shifted(own, "pos", -1)
    below = shifted(own, "pos", -TILE_COLS)
    diagonal = shifted(own, "pos", -(TILE_COLS + 1))
    bottom = jnp.concatenate([below, diagonal], axis=-1)
    region = jnp.concatenate([jnp.concatenate([own, right], axis=-1), bottom], axis=-2)
    place = lax.axis_index("pos")
    base_row = place // TILE_COLS * edge
    base_col = place % TILE_COLS * edge
    zero = jnp.zeros((), jnp.int32)

    def cut_window(row, col):
        return lax.dynamic_slice(region, (zero, zero, row, col), (SLICES, 2, size, size))

    local_rows = offsets[:, 0] - base_row
    local_cols = offsets[:, 1] - base_col
    windows = jax.vmap(cut_window)(local_rows, local_cols)

    def mode_total(values):
        return lax.psum(values, "mode")

    results = propagate(
        probe[0, 0],
        probe[0, 1],
        windows[:, 0, 0],
        windows[:, 0, 1],
        windows[:, 1, 0],
        windows[:, 1, 1],
        measured,
        mode_total,
        fresnel_phase,
    )
    front_obj_re, front_obj_im, back_obj_re, back_obj_im, probe_re_term, probe_im_term = results
    local_probe = jnp.stack([jnp.sum(probe_re_term, axis=0), jnp.sum(probe_im_term, axis=0)])[None]
    probe_grad = lax.psum(local_probe, "pos") / math.sqrt(count * lax.axis_size("pos"))
    terms = jnp.stack(
        [
            jnp.stack([front_obj_re, front_obj_im], axis=1),
            jnp.stack([back_obj_re, back_obj_im], axis=1),
        ],
        axis=1,
    )
    visits = terms.shape[0]

    def add_patch(step, total):
        start = (zero, zero, local_rows[step], local_cols[step])
        current = lax.dynamic_slice(total, start, (SLICES, 2, size, size))
        return lax.dynamic_update_slice(total, current + terms[step], start)

    extended = lax.fori_loop(0, visits, add_patch, jnp.zeros(region.shape, jnp.float32))
    core = extended[:, :, :edge, :edge]
    from_left = shifted(extended[:, :, :edge, edge:], "pos", 1)
    from_above = shifted(extended[:, :, edge:, :edge], "pos", TILE_COLS)
    from_diagonal = shifted(extended[:, :, edge:, edge:], "pos", TILE_COLS + 1)
    core = core.at[:, :, :, :size].add(from_left)
    core = core.at[:, :, :size, :].add(from_above)
    core = core.at[:, :, :size, :size].add(from_diagonal)
    object_part = lax.psum_scatter(core, "mode", scatter_dimension=2, tiled=True)
    return (object_part[None], probe_grad)


def solution(mesh):
    return jax.shard_map(
        body,
        mesh=mesh,
        in_specs=(
            P("pos", None, None, None, None),
            P("mode", None, None, None),
            P(),
            P("pos", None),
            P("pos", None, None),
        ),
        out_specs=(P("pos", None, None, "mode", None), P("mode", None, None, None)),
        check_vma=False,
    )
```

profile of v0, /device:TPU:1, one launch (start us, length us, event | category | flops | bytes accessed | tf_op | source)
XLA Modules:
  0.0 552.3 jit_solution(17968757601047624612)
XLA Ops:
  7.2 8.8 %collective-permute-start = (f32[2,2,128,128]{3,2,1,0:T(8,128)}, f32[2,2,128,128]{3,2,1,0:T(8,128)S(1)}, u32[]{:S(2)}, u32[]{:S(2)}) collective-permute-start(f32[2,2,128,128]{3,2,1,0:T(8,128)} %bitcast.275), channel_id=1, source_target_pairs={{4,0},{8,4},{12,8},{16,12},{20,16},{24,20},{28,24},{32,28},{36,32}... | collective-permute-start | bytes 786440 | tf_op jit(solution)/shard_map/ppermute | solution.py:15
  16.0 1.3 collective-permute-start.1
  17.3 1.3 collective-permute-start.2
  19.5 0.9 slice_bitcast_fusion.1
  20.9 14.5 %collective-permute-done.1 = f32[2,2,128,128]{3,2,1,0:T(8,128)S(1)} collective-permute-done((f32[2,2,128,128]{3,2,1,0:T(8,128)}, f32[2,2,128,128]{3,2,1,0:T(8,128)S(1)}, u32[]{:S(2)}, u32[]{:S(2)}) %collective-permute-start.1) | collective-permute-done | bytes 262176 | tf_op jit(solution)/shard_map/ppermute | solution.py:15
  35.3 6.7 %collective-permute-done.2 = f32[2,2,128,128]{3,2,1,0:T(8,128)S(1)} collective-permute-done((f32[2,2,128,128]{3,2,1,0:T(8,128)}, f32[2,2,128,128]{3,2,1,0:T(8,128)S(1)}, u32[]{:S(2)}, u32[]{:S(2)}) %collective-permute-start.2) | collective-permute-done | bytes 262176 | tf_op jit(solution)/shard_map/ppermute | solution.py:15
  42.1 8.3 %while.21 = (s32[]{:T(128)}, f32[2,2,256,256]{3,2,1,0:T(8,128)S(1)}, s32[4,4]{1,0:T(4,128)S(1)}, f32[4,2,2,128,128]{4,3,0,2,1:T(8,128)S(1)}, s32[]{:T(128)}) while((s32[]{:T(128)}, f32[2,2,256,256]{3,2,1,0:T(8,128)S(1)}, s32[4,4]{1,0:T(4,128)S(1)}, f32[4,2,2,128,128]{4,3,0,2,1:T(8,128)S(1)}, s32[]{:T(128)}) %tuple.89), condition=%wide.while_cond.3, body=%wide.while_body.3.sunk | while | flops 2 | bytes 524413 | solution.py:93
  42.7 1.4 bitcast_dynamic-update-slice_fusion.2
  44.8 1.4 bitcast_dynamic-update-slice_fusion.2
  46.9 1.4 bitcast_dynamic-update-slice_fusion.2
  48.9 1.4 bitcast_dynamic-update-slice_fusion.2
  50.4 0.8 fusion.99
  51.1 0.8 fusion.95
  51.9 0.8 fusion.11
  53.4 0.8 fusion.10
  56.4 0.8 fusion.87
  57.1 0.8 fusion.91
  57.9 0.8 fusion.8
  58.7 0.8 fusion.9
  61.7 13.5 %fusion.12 = (f32[4,128,128]{2,1,0:T(8,128)S(1)}, f32[4,128,128]{2,1,0:T(8,128)S(1)}, f32[4,128,128]{2,1,0:T(8,128)S(1)}) fusion(f32[4,128,128]{2,1,0:T(8,128)S(1)} %convolution_subtract_fusion.8, f32[4,2,2,128,128]{4,3,0,2,1:T(8,128)S(1)} %get-tuple-element.164, f32[4,128,128]{2,1,0:T(8,128)S(1)} %fusion.85, f32[4,128,128]{1,2,0:T(8,128)S(1)} %fusion.9), kind=kOutput, calls=%fused_computation.47 | convolution fusion | flops 101367808 | bytes 2097152 | tf_op jit(solution)/shard_map/...jk,kl->...jl/dot_general | solution.py:33
  80.2 1.5 multiply_add_fusion.1
  81.8 59.9 %all-reduce.3.cloned.1.call-done = f32[4,128,128]{2,1,0:T(8,128)} async-done(((f32[4,128,128]{2,1,0:T(8,128)}), f32[4,128,128]{2,1,0:T(8,128)}) %all-reduce.3.cloned.1.call-update) | async-done | bytes 262160 | tf_op jit(solution)/shard_map/psum | solution.py:100
  141.6 1.0 sub.124
  142.6 0.7 fusion.26
  143.4 0.7 fusion.22
  144.1 0.7 fusion.5
  144.9 0.7 fusion.4
  147.8 0.8 fusion.14
  153.7 0.9 convolution_subtract_fusion.2
  154.6 0.8 fusion.61
  155.4 0.8 fusion.57
  156.1 0.8 fusion.1
  156.9 0.8 fusion
  159.9 0.8 fusion.19
  160.9 32.3 %while.20 = (s32[]{:T(128)}, f32[2,2,256,256]{3,2,1,0:T(8,128)S(1)}, s32[4]{0:T(128)S(1)}, s32[4]{0:T(128)S(1)}, f32[4,2,2,128,128]{4,3,0,2,1:T(8,128)S(1)}, /*index=5*/s32[]{:T(128)}, s32[]{:T(128)}, s32[]{:T(128)}) while((s32[]{:T(128)}, f32[2,2,256,256]{3,2,1,0:T(8,128)S(1)}, s32[4]{0:T(128)S(1)}, s32[4]{0:T(128)S(1)}, ...), condition=%wide.region_2.3_spmd, body=%wide.region_1.2_spmd.sunk | while | flops 65544 | bytes 1310913 | solution.py:130
  166.2 3.0 dynamic_update_slice.8
  174.5 1.8 dynamic_update_slice.8
  181.5 3.1 dynamic_update_slice.8
  189.9 3.4 dynamic_update_slice.8
  193.3 6.0 %collective-permute-start.3 = (f32[2,2,128,128]{3,2,1,0:T(8,128)S(1)}, f32[2,2,128,128]{3,2,1,0:T(8,128)S(1)}, u32[]{:S(2)}, u32[]{:S(2)}) collective-permute-start(f32[2,2,128,128]{3,2,1,0:T(8,128)S(1)} %get-tuple-element.201), channel_id=1, source_target_pairs={{0,4},{4,8},{8,12},{12,16},{16,20},{20,24},{24,28},{28,32},{32,36}... | collective-permute-start | bytes 786440 | tf_op jit(solution)/shard_map/ppermute | solution.py:15
  199.4 4.1 collective-permute-start.4
  203.4 5.5 collective-permute-start.5
  209.6 1.6 collective-permute-done.4
  211.2 15.5 %collective-permute-done.5 = f32[2,2,128,128]{3,2,1,0:T(8,128)S(1)} collective-permute-done((f32[2,2,128,128]{3,2,1,0:T(8,128)S(1)}, f32[2,2,128,128]{3,2,1,0:T(8,128)S(1)}, u32[]{:S(2)}, u32[]{:S(2)}) %collective-permute-start.5) | collective-permute-done | bytes 262176 | tf_op jit(solution)/shard_map/ppermute | solution.py:15
  226.7 0.8 add_add_fusion
  227.5 294.9 %all-reduce.5.cloned.1.call-done = f32[1,2,128,128]{3,2,1,0:T(8,128)} async-done(((f32[1,2,128,128]{3,2,1,0:T(8,128)}), f32[1,2,128,128]{3,2,1,0:T(8,128)}) %all-reduce.5.cloned.1.call-update) | async-done | bytes 131088 | tf_op jit(solution)/shard_map/psum | solution.py:115
  522.5 1.6 broadcast_multiply_fusion
  524.0 21.3 %reduce-scatter.2.cloned.1.call-done = f32[2,2,32,128]{3,2,1,0:T(8,128)} async-done(((f32[2,2,128,128]{3,2,1,0:T(8,128)}), f32[2,2,32,128]{3,2,1,0:T(8,128)}) %reduce-scatter.2.cloned.1.call-update) | async-done | bytes 65552 | tf_op jit(solution)/shard_map/reduce_scatter | solution.py:138
  (79 shorter events, 29.8 us)
Async XLA Ops:
  7.2 134.5 %all-reduce.3.cloned.1.call-start = ((), (), s32[]{:S(2)}) async-start(), calls=%async_computation.1 | async-start | bytes 524288 | tf_op jit(solution)/shard_map/psum | solution.py:100
  7.2 13.6 %collective-permute-start = (f32[2,2,128,128]{3,2,1,0:T(8,128)}, f32[2,2,128,128]{3,2,1,0:T(8,128)S(1)}, u32[]{:S(2)}, u32[]{:S(2)}) collective-permute-start(f32[2,2,128,128]{3,2,1,0:T(8,128)} %bitcast.275), channel_id=1, source_target_pairs={{4,0},{8,4},{12,8},{16,12},{20,16},{24,20},{28,24},{32,28},{36,32}... | collective-permute-start | bytes 786440 | tf_op jit(solution)/shard_map/ppermute | solution.py:15
  16.0 19.3 %collective-permute-start.1 = (f32[2,2,128,128]{3,2,1,0:T(8,128)}, f32[2,2,128,128]{3,2,1,0:T(8,128)S(1)}, u32[]{:S(2)}, u32[]{:S(2)}) collective-permute-start(f32[2,2,128,128]{3,2,1,0:T(8,128)} %bitcast.276), channel_id=1, source_target_pairs={{16,0},{20,4},{24,8},{28,12},{32,16},{36,20},{40,24},{44,28},{48,3... | collective-permute-start | bytes 786440 | tf_op jit(solution)/shard_map/ppermute | solution.py:15
  17.3 24.7 %collective-permute-start.2 = (f32[2,2,128,128]{3,2,1,0:T(8,128)}, f32[2,2,128,128]{3,2,1,0:T(8,128)S(1)}, u32[]{:S(2)}, u32[]{:S(2)}) collective-permute-start(f32[2,2,128,128]{3,2,1,0:T(8,128)} %bitcast.277), channel_id=1, source_target_pairs={{20,0},{24,4},{28,8},{32,12},{36,16},{40,20},{44,24},{48,28},{52,3... | collective-permute-start | bytes 786440 | tf_op jit(solution)/shard_map/ppermute | solution.py:15
  18.6 0.7 copy-start.3
  18.6 2.0 copy-start.2
  18.6 23.4 %copy-start.1 = (f32[1,2,2,128,128]{4,3,2,1,0:T(8,128)S(1)}, f32[1,2,2,128,128]{4,3,2,1,0:T(8,128)}, u32[]{:S(2)}) copy-start(f32[1,2,2,128,128]{4,3,2,1,0:T(8,128)} %param.19) | copy-start | bytes 786436
  81.7 59.9 %copy-start = (f32[4,128,128]{2,1,0:T(8,128)S(1)}, f32[4,128,128]{2,1,0:T(8,128)}, u32[]{:S(2)}) copy-start(f32[4,128,128]{2,1,0:T(8,128)} %param.23) | copy-start | bytes 786436
  81.7 440.7 %all-reduce.5.cloned.1.call-start = ((), (), s32[]{:S(2)}) async-start(), calls=%async_computation.3 | async-start | bytes 262144 | tf_op jit(solution)/shard_map/psum | solution.py:115
  193.3 16.3 %collective-permute-start.3 = (f32[2,2,128,128]{3,2,1,0:T(8,128)S(1)}, f32[2,2,128,128]{3,2,1,0:T(8,128)S(1)}, u32[]{:S(2)}, u32[]{:S(2)}) collective-permute-start(f32[2,2,128,128]{3,2,1,0:T(8,128)S(1)} %get-tuple-element.201), channel_id=1, source_target_pairs={{0,4},{4,8},{8,12},{12,16},{16,20},{20,24},{24,28},{28,32},{32,36}... | collective-permute-start | bytes 786440 | tf_op jit(solution)/shard_map/ppermute | solution.py:15
  199.4 11.9 %collective-permute-start.4 = (f32[2,2,128,128]{3,2,1,0:T(8,128)S(1)}, f32[2,2,128,128]{3,2,1,0:T(8,128)S(1)}, u32[]{:S(2)}, u32[]{:S(2)}) collective-permute-start(f32[2,2,128,128]{3,2,1,0:T(8,128)S(1)} %get-tuple-element.203), channel_id=1, source_target_pairs={{0,16},{4,20},{8,24},{12,28},{16,32},{20,36},{24,40},{28,44},{32,4... | collective-permute-start | bytes 786440 | tf_op jit(solution)/shard_map/ppermute | solution.py:15
  203.4 23.3 %collective-permute-start.5 = (f32[2,2,128,128]{3,2,1,0:T(8,128)S(1)}, f32[2,2,128,128]{3,2,1,0:T(8,128)S(1)}, u32[]{:S(2)}, u32[]{:S(2)}) collective-permute-start(f32[2,2,128,128]{3,2,1,0:T(8,128)S(1)} %get-tuple-element.202), channel_id=1, source_target_pairs={{0,20},{4,24},{8,28},{12,32},{16,36},{20,40},{24,44},{28,48},{32,5... | collective-permute-start | bytes 786440 | tf_op jit(solution)/shard_map/ppermute | solution.py:15
  209.6 335.8 %reduce-scatter.2.cloned.1.call-start = ((), (), s32[]{:S(2)}) async-start(), calls=%async_computation.2 | async-start | bytes 327680 | tf_op jit(solution)/shard_map/reduce_scatter | solution.py:138
Sparse Core Ops, SparseCore 0:
  81.8 59.7 all-reduce.2
  209.7 312.7 all-reduce.4
  526.1 19.2 reduce-scatter.1
where the time goes:
time: 563 us; the launch traced here: 552 us
  waiting for transfers between devices  414 us (74%)
  matrix products  49.1 us (9%)
  starting transfers between devices  27 us (5%)
  local copies, waits for them, and re-layouts  26.3 us (5%)
  loops' own time  15.8 us (3%)
  between operations  14.6 us (3%)
    psum x1, waiting for transfers between devices, body(): lax.psum(local_probe, 'pos') / math.sqrt(count * lax.axis_size('pos'))  295 us
    psum x1, waiting for transfers between devices, mode_total(): return lax.psum(values, 'mode')  59.9 us
    ppermute x6, waiting for transfers between devices, shifted(): lax.ppermute(value, axis, [(source, source + steps) for source in range(i...  38.3 us
    dot_general x24, matrix products, right_side(): return jnp.einsum('...jk,kl->...jl', data, table, precision=highest)  31.1 us
    ppermute x6, starting transfers between devices, shifted(): lax.ppermute(value, axis, [(source, source + steps) for source in range(i...  26.9 us
    reduce_scatter x1, waiting for transfers between devices, body(): lax.psum_scatter(core, 'mode', scatter_dimension=2, tiled=True)  21.3 us
    dot_general x24, matrix products, left_side(): return jnp.einsum('jk,...kl->...jl', table, data, precision=highest)  17.9 us
    another operation x1, loops' own time, body(): lax.fori_loop(0, visits, add_patch, jnp.zeros(region.shape, jnp.float32))  15.7 us
  transfers between devices with their start and end apart: 9, of which 7 were waited for; matrix products, arithmetic and copies ran while one was open for 1% of the time, Pallas kernels for 0%

commit v1 on v0

v1 whole, which is shorter than its diff:
```python
import math

import jax
import jax.numpy as jnp
import numpy as np
from jax import lax
from jax.experimental import pallas as pl
from jax.experimental.pallas import tpu as pltpu
from jax.sharding import PartitionSpec as P

NX, NY, NZ, NC = 4, 4, 16, 2
NP = NY * NZ * NC
COLS = 4
S = 128
Q = S // NX
F32 = jnp.float32
BF16 = jnp.bfloat16
HALO = (1, COLS, COLS + 1)


def dft_tables():
    k = np.arange(S)
    angle = (np.outer(k, k) % S) * (2.0 * np.pi / S)
    cos, sin = np.cos(angle) / math.sqrt(S), np.sin(angle) / math.sqrt(S)
    fwd = np.block([[cos, -sin], [sin, cos]])
    out = []
    for table in (fwd, fwd.T):
        table = table.astype(np.float32)
        hi = table.astype(BF16)
        lo = (table - hi.astype(np.float32)).astype(BF16)
        out.append(np.stack([hi, lo]))
    return np.stack(out)


def split(x):
    hi = x.astype(BF16)
    return hi, (x - hi.astype(F32)).astype(BF16)


def dot(a, b):
    return jnp.dot(a, b, preferred_element_type=F32)


def mul(a, b):
    return a[0] * b[0] - a[1] * b[1], a[0] * b[1] + a[1] * b[0]


def cmul(a, b):
    return a[0] * b[0] + a[1] * b[1], a[0] * b[1] - a[1] * b[0]


def kernel(
    tiles, probe, phase, offs, measured, tables,
    out_obj, out_probe,
    quarter, rows_sel, win, praw, prb, ph, hc, hs, meas, tab, psi, far, obj, rxo, hsend, hown, hrecv,
    pg, rxc, rxy, zs, rxz, gz, pgall,
    load_sem, halo_s, halo_r, a2a_s, a2a_r, pag_s, pag_r, pfw_s, pfw_r,
    oa_s, oa_r, oh_s, oh_r, c_s, c_r, xy_s, xy_r, z_s, z_r, zg_s, zg_r, f_s, f_r,
):
    p = lax.axis_index("pos")
    m = lax.axis_index("mode")
    c = lax.rem(p, NC)
    z = lax.rem(p // NC, NZ)
    y = p // (NC * NZ)

    def at(yy, zz, cc):
        return (yy * NZ + zz) * NC + cc

    def pos_plus(d):
        return lax.rem(p + (d + NP), NP)

    def mode_plus(d):
        return lax.rem(m + (d + NX), NX)

    def remote(src, dst, ss, rs, pos, mode):
        return pltpu.make_async_remote_copy(
            src_ref=src, dst_ref=dst, send_sem=ss, recv_sem=rs,
            device_id=(pos, mode), device_id_type=pl.DeviceIdType.MESH,
        )

    def band(k):
        return pl.ds(pl.multiple_of(k * Q, Q), Q)

    mine = band(m)
    loads = [
        pltpu.make_async_copy(tiles.at[0, :, :, mine, :], quarter.at[:, 0], load_sem.at[0]),
        pltpu.make_async_copy(probe.at[0], praw.at[m], load_sem.at[1]),
        pltpu.make_async_copy(phase, ph, load_sem.at[2]),
        pltpu.make_async_copy(measured.at[m], meas, load_sem.at[3]),
        pltpu.make_async_copy(tables, tab, load_sem.at[4]),
    ]
    for copy in loads:
        copy.start()

    partners = []
    for d in HALO:
        partners += [(pos_plus(d), m), (pos_plus(-d), m)]
    for dx in range(NX):
        for dy in range(NY):
            if dx or dy:
                partners.append((at(lax.rem(y + dy, NY), z, c), mode_plus(dx)))
    for d in range(1, NZ):
        partners.append((at(y, lax.rem(z + d, NZ), c), m))
    for dy in range(1, NY):
        partners.append((at(lax.rem(y + dy, NY), z, 1 - c), m))
    barrier = pltpu.get_barrier_semaphore()
    for pos, mode in partners:
        pl.semaphore_signal(barrier, inc=1, device_id=(pos, mode), device_id_type=pl.DeviceIdType.MESH)
    pl.semaphore_wait(barrier, len(partners))

    started = []

    def go(copy):
        copy.start()
        started.append(copy)
        return copy

    halo = [[None] * 3 for _ in range(2)]
    for s in range(2):
        for h in (2, 1, 0):
            halo[s][h] = go(remote(
                tiles.at[0, s, :, mine, :], quarter.at[s, h + 1], halo_s.at[s, h], halo_r.at[s, h],
                pos_plus(-HALO[h]), m,
            ))
        if s == 0:
            pag = [
                go(remote(probe.at[0, c], praw.at[m, c], pag_s.at[d - 1], pag_r.at[d - 1], p, mode_plus(d)))
                for d in range(1, NX)
            ]

    base_row = p // COLS * S
    base_col = lax.rem(p, COLS) * S
    iota_r = lax.broadcasted_iota(jnp.int32, (Q, S), 0) + m * Q
    iota_c = lax.broadcasted_iota(jnp.int32, (Q, S), 1)

    def corner(k):
        return offs[k, 0] - base_row, offs[k, 1] - base_col

    row0, col0 = corner(m)
    row_back, col_back = lax.rem(S - row0, S), lax.rem(S - col0, S)

    loads[2].wait()
    hc[...] = jnp.cos(ph[...])
    hs[...] = jnp.sin(ph[...])
    loads[0].wait()

    a2a = [[None] * 3 for _ in range(2)]

    def window_bands(s):
        for h in range(3):
            halo[s][h].wait_recv()
        for k in range(NX):
            r, cc = corner(k)
            for plane in range(2):
                upper = jnp.where(iota_c >= cc, quarter[s, 0, plane], quarter[s, 1, plane])
                lower = jnp.where(iota_c >= cc, quarter[s, 2, plane], quarter[s, 3, plane])
                rows_sel[s, k, plane] = jnp.where(iota_r >= r, upper, lower)
        for d in range(1, NX):
            k = mode_plus(d)
            a2a[s][d - 1] = go(remote(
                rows_sel.at[s, k], win.at[s, :, mine, :], a2a_s.at[s, d - 1], a2a_r.at[s, d - 1], p, k,
            ))
        win[s, :, mine, :] = rows_sel[s, m]

    window_bands(0)

    loads[1].wait()
    pfw = []
    for d in range(1, NX):
        pag[d - 1].wait_recv()
        k = mode_plus(-d)
        pfw.append(go(remote(
            praw.at[k, c], praw.at[k, c], pfw_s.at[d - 1], pfw_r.at[d - 1], at(y, z, 1 - c), m,
        )))
    window_bands(1)
    for copy in pfw:
        copy.wait_recv()
    for k in range(NX):
        for plane in range(2):
            prb[k, plane] = pltpu.roll(pltpu.roll(praw[k, plane], row0, 0), col0, 1)

    loads[3].wait()
    loads[4].wait()

    def transform(a, b, inverse):
        right, left = (1, 0) if inverse else (0, 1)
        x = jnp.concatenate([jnp.concatenate(a, axis=1), jnp.concatenate(b, axis=1)], axis=0)
        hi, lo = split(x)
        w_hi, w_lo = tab[right, 0], tab[right, 1]
        o = dot(hi, w_hi) + (dot(lo, w_hi) + dot(hi, w_lo))
        x = jnp.concatenate(
            [
                jnp.concatenate([o[:S, :S], o[S:, :S]], axis=1),
                jnp.concatenate([o[:S, S:], o[S:, S:]], axis=1),
            ],
            axis=0,
        )
        hi, lo = split(x)
        w_hi, w_lo = tab[left, 0], tab[left, 1]
        o = dot(w_hi, hi) + (dot(w_hi, lo) + dot(w_lo, hi))
        return (o[:S, :S], o[S:, :S]), (o[:S, S:], o[S:, S:])

    def both(ref, k):
        return ref[k, 0], ref[k, 1]

    def put(ref, k, value):
        ref[k, 0] = value[0]
        ref[k, 1] = value[1]

    pairs = ((0, 1), (2, 3))
    for d in range(1, NX):
        a2a[0][d - 1].wait_recv()
    for pair in pairs:
        spec = transform(*[mul(both(prb, k), both(win, 0)) for k in pair], False)
        wave = transform(*[mul(v, (hc[...], hs[...])) for v in spec], True)
        for k, v in zip(pair, wave):
            put(psi, k, v)
    for d in range(1, NX):
        a2a[1][d - 1].wait_recv()
    for pair in pairs:
        wave = transform(*[mul(both(psi, k), both(win, 1)) for k in pair], False)
        for k, v in zip(pair, wave):
            put(far, k, v)
    total = -meas[...]
    for k in range(NX):
        total = total + (far[k, 0] * far[k, 0] + far[k, 1] * far[k, 1])
    meas[...] = total
    for pair in pairs:
        grad = transform(*[(meas[...] * far[k, 0], meas[...] * far[k, 1]) for k in pair], True)
        for k, v in zip(pair, grad):
            put(far, k, v)

    oa = [[None] * 3 for _ in range(2)]

    def send_object(s):
        for d in range(1, NX):
            k = mode_plus(d)
            oa[s][d - 1] = go(remote(
                obj.at[s, :, band(k), :], rxo.at[s, d - 1], oa_s.at[s, d - 1], oa_r.at[s, d - 1], p, k,
            ))

    terms = [cmul(both(psi, k), both(far, k)) for k in range(NX)]
    for plane in range(2):
        obj[1, plane] = (terms[0][plane] + terms[1][plane]) + (terms[2][plane] + terms[3][plane])
    send_object(1)

    cc_copies = [None] * NX
    for index, pair in enumerate(pairs):
        spec = transform(*[cmul(both(win, 1), both(far, k)) for k in pair], False)
        first = transform(*[cmul((hc[...], hs[...]), v) for v in spec], True)
        for k, v in zip(pair, first):
            put(far, k, v)
            back = cmul(both(win, 0), v)
            for plane in range(2):
                pg[k, plane] = pltpu.roll(pltpu.roll(back[plane], row_back, 0), col_back, 1)
            cc_copies[k] = go(remote(
                pg.at[k, 1 - c], rxc.at[k], c_s.at[k], c_r.at[k], at(y, z, 1 - c), m,
            ))
    terms = [cmul(both(prb, k), both(far, k)) for k in range(NX)]
    for plane in range(2):
        obj[0, plane] = (terms[0][plane] + terms[1][plane]) + (terms[2][plane] + terms[3][plane])
    send_object(0)

    guarded = []

    def guarded_go(cond, make):
        @pl.when(cond)
        def _():
            make().start()

        guarded.append((cond, make))

    for k in range(NX):
        cc_copies[k].wait_recv()
        pg[k, c] = pg[k, c] + rxc[k]
        dx = lax.rem(k - m + NX, NX)
        for dy in range(NY):
            yy = lax.rem(y + dy, NY)

            def make(k=k, dx=dx, dy=dy, yy=yy):
                return remote(
                    pg.at[k, c, band(yy), :], rxy.at[dx, dy], xy_s.at[dx, dy], xy_r.at[dx, dy], at(yy, z, c), k,
                )

            if dy:
                go(make())
            else:
                guarded_go(k != m, make)

    oh = [[None] * 3 for _ in range(2)]

    def spread_object(s):
        for d in range(1, NX):
            oa[s][d - 1].wait_recv()
        sums = [[None, None] for _ in range(4)]
        for d in range(NX):
            r, cc = corner(mode_plus(-d))
            low, high = iota_r >= r, iota_c >= cc
            for plane in range(2):
                v = rxo[s, d - 1, plane] if d else obj[s, plane, mine, :]
                zero = jnp.zeros_like(v)
                upper, lower = jnp.where(low, v, zero), jnp.where(low, zero, v)
                parts = (
                    jnp.where(high, upper, zero), jnp.where(high, zero, upper),
                    jnp.where(high, lower, zero), jnp.where(high, zero, lower),
                )
                for i in range(4):
                    old = sums[i][plane]
                    sums[i][plane] = parts[i] if old is None else old + parts[i]
        for plane in range(2):
            hown[s, plane] = sums[0][plane]
            for h in range(3):
                hsend[s, h, plane] = sums[h + 1][plane]
        for h in (2, 1, 0):
            oh[s][h] = go(remote(
                hsend.at[s, h], hrecv.at[s, h], oh_s.at[s, h], oh_r.at[s, h], pos_plus(HALO[h]), m,
            ))

    spread_object(1)
    spread_object(0)

    def wait_recv_xy(dx, dy):
        remote(rxy.at[dx, dy], rxy.at[dx, dy], xy_s.at[dx, dy], xy_r.at[dx, dy], p, m).wait_recv()

    part = pg[m, c, band(y), :]
    for dx in range(NX):
        for dy in range(NY):
            if dx or dy:
                wait_recv_xy(dx, dy)
                part = part + rxy[dx, dy]
    for i in range(4):
        zs[i] = part[8 * i : 8 * i + 8]

    owner = lax.rem(z, 4) == 0
    own = z // 4
    for i in range(4):
        d = lax.rem(4 * i - z + NZ, NZ)

        def make(i=i, d=d):
            return remote(zs.at[i], rxz.at[d], z_s.at[i], z_r.at[d], at(y, 4 * i, c), m)

        guarded_go(z != 4 * i, make)

    def z_gather(d):
        return remote(gz.at[own], gz.at[own], zg_s.at[d], zg_r.at[own], at(y, lax.rem(z + d, NZ), c), m)

    @pl.when(owner)
    def _():
        full = zs[own]
        for d in range(1, NZ):
            remote(rxz.at[d], rxz.at[d], z_s.at[0], z_r.at[d], p, m).wait_recv()
            full = full + rxz[d]
        gz[own] = full * (1.0 / math.sqrt(NX * NP))
        for d in range(1, NZ):
            z_gather(d).start()

    for s in range(2):
        for h in range(3):
            oh[s][h].wait_recv()
        for plane in range(2):
            out_obj[0, s, plane] = (hown[s, plane] + hrecv[s, 0, plane]) + (hrecv[s, 1, plane] + hrecv[s, 2, plane])

    for i in range(4):
        @pl.when(z != 4 * i)
        def _(i=i):
            remote(gz.at[i], gz.at[i], zg_s.at[0], zg_r.at[i], p, m).wait_recv()

    for i in range(4):
        pgall[c, y, i] = gz[i]
    last = []
    for dc in range(NC):
        for dy in range(NY):
            if dc or dy:
                yy = lax.rem(y + dy, NY)
                cc = lax.rem(c + dc, NC)
                last.append(go(remote(
                    gz, pgall.at[c, y], f_s.at[dc, dy], f_r.at[dc, dy], at(yy, z, cc), m,
                )))
    for copy in last:
        copy.wait_recv()
    for plane in range(2):
        for yy in range(NY):
            for i in range(4):
                out_probe[0, plane, yy * Q + 8 * i : yy * Q + 8 * i + 8] = pgall[plane, yy, i]

    for copy in started:
        copy.wait_send()
    for cond, make in guarded:
        @pl.when(cond)
        def _(make=make):
            make().wait_send()

    @pl.when(owner)
    def _():
        for d in range(1, NZ):
            z_gather(d).wait_send()


def body(tables, tiles, probe, phase, offs, measured):
    any_space = pl.BlockSpec(memory_space=pl.ANY)
    vmem = pltpu.VMEM
    dma = pltpu.SemaphoreType.DMA
    return pl.pallas_call(
        kernel,
        out_shape=(
            jax.ShapeDtypeStruct((1, 2, 2, Q, S), F32),
            jax.ShapeDtypeStruct((1, 2, S, S), F32),
        ),
        in_specs=[any_space, any_space, any_space, pl.BlockSpec(memory_space=pltpu.SMEM), any_space, any_space],
        out_specs=(pl.BlockSpec(memory_space=vmem), pl.BlockSpec(memory_space=vmem)),
        scratch_shapes=[
            vmem((2, 4, 2, Q, S), F32),
            vmem((2, NX, 2, Q, S), F32),
            vmem((2, 2, S, S), F32),
            vmem((NX, 2, S, S), F32),
            vmem((NX, 2, S, S), F32),
            vmem((S, S), F32),
            vmem((S, S), F32),
            vmem((S, S), F32),
            vmem((S, S), F32),
            vmem((2, 2, 2 * S, 2 * S), BF16),
            vmem((NX, 2, S, S), F32),
            vmem((NX, 2, S, S), F32),
            vmem((2, 2, S, S), F32),
            vmem((2, 3, 2, Q, S), F32),
            vmem((2, 3, 2, Q, S), F32),
            vmem((2, 2, Q, S), F32),
            vmem((2, 3, 2, Q, S), F32),
            vmem((NX, 2, S, S), F32),
            vmem((NX, S, S), F32),
            vmem((NX, NY, Q, S), F32),
            vmem((4, 8, S), F32),
            vmem((NZ, 8, S), F32),
            vmem((4, 8, S), F32),
            vmem((NC, NY, 4, 8, S), F32),
            dma((5,)),
            dma((2, 3)), dma((2, 3)), dma((2, 3)), dma((2, 3)),
            dma((3,)), dma((3,)), dma((3,)), dma((3,)),
            dma((2, 3)), dma((2, 3)), dma((2, 3)), dma((2, 3)),
            dma((NX,)), dma((NX,)), dma((NX, NY)), dma((NX, NY)),
            dma((4,)), dma((NZ,)), dma((NZ,)), dma((4,)),
            dma((NC, NY)), dma((NC, NY)),
        ],
        compiler_params=pltpu.CompilerParams(
            collective_id=0, has_side_effects=True, vmem_limit_bytes=32 * 1024 * 1024
        ),
    )(tiles, probe, phase, offs, measured, tables)


def solution(mesh):
    tables = dft_tables()

    def run(tiles, probe, phase, offs, measured):
        return jax.shard_map(
            lambda *args: body(jnp.asarray(tables), *args),
            mesh=mesh,
            in_specs=(
                P("pos", None, None, None, None),
                P("mode", None, None, None),
                P(),
                P("pos", None),
                P("pos", None, None),
            ),
            out_specs=(P("pos", None, None, "mode", None), P("mode", None, None, None)),
            check_vma=False,
        )(tiles, probe, phase, offs, measured)

    return run
```

time: 563 us -> 71.4 us (0.13); the launches traced: 552 us -> 71.1 us
  waiting for transfers between devices: 414 us -> 0 us
  Pallas kernels: 0 us -> 63.8 us
  matrix products: 49.1 us -> 0 us
  starting transfers between devices: 27 us -> 0 us
  local copies, waits for them, and re-layouts: 26.3 us -> 6.74 us
  loops' own time: 15.8 us -> 0 us
  between operations: 14.6 us -> 0.64 us
    psum x2 -> x0, waiting for transfers between devices: 355 us -> none  [the longest x1 295 us: body(): lax.psum(local_probe, 'pos') / math.sqrt(count * lax.axis_size('pos'))]
    pallas_call x0 -> x1, Pallas kernels: none -> 63.8 us  [body(): pl.pallas_call(kernel, out_shape=(jax.ShapeDtypeStruct((1, 2, 2, Q, S), F...]
    dot_general x48 -> x0, matrix products: 49.1 us -> none  [the longest x24 31.1 us: right_side(): return jnp.einsum('...jk,kl->...jl', data, table, precision=highest)]
    ppermute x6 -> x0, waiting for transfers between devices: 38.3 us -> none  [shifted(): lax.ppermute(value, axis, [(source, source + steps) for source in range(i...]
    ppermute x6 -> x0, starting transfers between devices: 26.9 us -> none  [shifted(): lax.ppermute(value, axis, [(source, source + steps) for source in range(i...]
    reduce_scatter x1 -> x0, waiting for transfers between devices: 21.3 us -> none  [body(): lax.psum_scatter(core, 'mode', scatter_dimension=2, tiled=True)]
    another operation x2 -> x0, loops' own time: 15.8 us -> none  [the longest x1 15.7 us: body(): lax.fori_loop(0, visits, add_patch, jnp.zeros(region.shape, jnp.float32))]
    dynamic_update_slice x4 -> x0, local copies, waits for them, and re-layouts: 11.3 us -> none  [add_patch(): return lax.dynamic_update_slice(total, current + terms[step], start)]
  transfers between devices with their start and end apart: 9 -> 0, of which waited for: 7 -> 0; matrix products, arithmetic and copies ran while one was open for 1% -> 0% of each run, Pallas kernels for 0% -> 0%
where the time goes in v1:
time: 71.4 us; the launch traced here: 71.1 us
  Pallas kernels  63.8 us (89%)
  local copies, waits for them, and re-layouts  6.74 us (9%)
    pallas_call x1, Pallas kernels, body(): pl.pallas_call(kernel, out_shape=(jax.ShapeDtypeStruct((1, 2, 2, Q, S), F...  63.8 us
    unnamed x13, local copies, waits for them, and re-layouts  6.74 us

profile of v1, /device:TPU:1, one launch (start us, length us, event | category | flops | bytes accessed | tf_op | source)
XLA Modules:
  0.0 71.1 jit_solution(385151191046350517)
XLA Ops:
  0.6 0.8 %copy.8.offs = s32[4,2]{1,0:T(4,128)S(1)} copy(s32[4,2]{0,1:T(2,128)} %param.9) | data formatting | bytes 64 | tf_op args[3]
  1.4 0.0 copy-start
  1.4 1.0 %copy-done = bf16[2,2,256,256]{3,2,1,0:T(8,128)(2,1)S(1)} copy-done((bf16[2,2,256,256]{3,2,1,0:T(8,128)(2,1)S(1)}, bf16[2,2,256,256]{3,2,1,0:T(8,128)(2,1)}, u32[]{:S(2)}) %copy-start) | copy-done | bytes 524312
  2.4 0.0 copy-start.1
  2.4 0.9 %copy-done.1 = f32[1,2,2,128,128]{4,3,2,1,0:T(8,128)S(1)} copy-done((f32[1,2,2,128,128]{4,3,2,1,0:T(8,128)S(1)}, f32[1,2,2,128,128]{4,3,2,1,0:T(8,128)}, u32[]{:S(2)}) %copy-start.1) | copy-done | bytes 262168
  3.4 0.0 copy-start.2
  3.4 0.9 %copy-done.2 = f32[4,128,128]{2,1,0:T(8,128)S(1)} copy-done((f32[4,128,128]{2,1,0:T(8,128)S(1)}, f32[4,128,128]{2,1,0:T(8,128)}, u32[]{:S(2)}) %copy-start.2) | copy-done | bytes 262168
  4.3 0.0 copy-start.3
  4.3 0.9 %copy-done.3 = f32[1,2,128,128]{3,2,1,0:T(8,128)S(1)} copy-done((f32[1,2,128,128]{3,2,1,0:T(8,128)S(1)}, f32[1,2,128,128]{3,2,1,0:T(8,128)}, u32[]{:S(2)}) %copy-start.3) | copy-done | bytes 131096
  5.2 0.0 copy-start.4
  5.2 0.8 %copy-done.4 = f32[128,128]{1,0:T(8,128)S(1)} copy-done((f32[128,128]{1,0:T(8,128)S(1)}, f32[128,128]{1,0:T(8,128)}, u32[]{:S(2)}) %copy-start.4) | copy-done | bytes 65560
  6.1 63.8 %shard_map.77 = (f32[1,2,2,32,128]{4,3,2,1,0:T(8,128)S(1)}, f32[1,2,128,128]{3,2,1,0:T(8,128)S(1)}) custom-call(f32[1,2,2,128,128]{4,3,2,1,0:T(8,128)S(1)} %copy-done.1, f32[1,2,128,128]{3,2,1,0:T(8,128)S(1)} %copy-done.3, f32[128,128]{1,0:T(8,128)S(1)} %copy-done.4, s32[4,2]{1,0:T(4,128)S(1)} %copy.8.offs, f32[4,128,128]{2,1,0:T(8,128)S(1)} %copy-done.2, ...), custom_call_target="tpu_custom_call" | custom-call | tf_op jit(solution)/shard_map/pallas_call | solution.py:403
  69.9 0.6 copy.11
  70.5 0.7 copy.12
Async XLA Ops:
  1.4 1.0 %copy-start = (bf16[2,2,256,256]{3,2,1,0:T(8,128)(2,1)S(1)}, bf16[2,2,256,256]{3,2,1,0:T(8,128)(2,1)}, u32[]{:S(2)}) copy-start(bf16[2,2,256,256]{3,2,1,0:T(8,128)(2,1)} %constant.2.clone.tables) | copy-start | bytes 1572868
  2.4 0.9 %copy-start.1 = (f32[1,2,2,128,128]{4,3,2,1,0:T(8,128)S(1)}, f32[1,2,2,128,128]{4,3,2,1,0:T(8,128)}, u32[]{:S(2)}) copy-start(f32[1,2,2,128,128]{4,3,2,1,0:T(8,128)} %tiles.1) | copy-start | bytes 786436
  3.4 0.9 %copy-start.2 = (f32[4,128,128]{2,1,0:T(8,128)S(1)}, f32[4,128,128]{2,1,0:T(8,128)}, u32[]{:S(2)}) copy-start(f32[4,128,128]{2,1,0:T(8,128)} %measured.1) | copy-start | bytes 786436
  4.3 0.9 %copy-start.3 = (f32[1,2,128,128]{3,2,1,0:T(8,128)S(1)}, f32[1,2,128,128]{3,2,1,0:T(8,128)}, u32[]{:S(2)}) copy-start(f32[1,2,128,128]{3,2,1,0:T(8,128)} %probe.1) | copy-start | bytes 393220
  5.2 0.8 %copy-start.4 = (f32[128,128]{1,0:T(8,128)S(1)}, f32[128,128]{1,0:T(8,128)}, u32[]{:S(2)}) copy-start(f32[128,128]{1,0:T(8,128)} %phase.1) | copy-start | bytes 196612

commit v2 on v1

--- a/solution.py
+++ b/solution.py
@@ -50,12 +50,12 @@
 
 
 def kernel(
-    tiles, probe, phase, offs, measured, tables,
+    tiles, probe, phase, corners, measured, tables,
     out_obj, out_probe,
-    quarter, rows_sel, win, praw, prb, ph, hc, hs, meas, tab, psi, far, obj, rxo, hsend, hown, hrecv,
-    pg, rxc, rxy, zs, rxz, gz, pgall,
-    load_sem, halo_s, halo_r, a2a_s, a2a_r, pag_s, pag_r, pfw_s, pfw_r,
-    oa_s, oa_r, oh_s, oh_r, c_s, c_r, xy_s, xy_r, z_s, z_r, zg_s, zg_r, f_s, f_r,
+    offs, quarter, rows_sel, win, praw, prb, ph, hc, hs, meas, tab, psi, far, obj, rxo, hsend, hown, hrecv,
+    pg, rxc, rxy, zs, pgall,
+    load_sem, round1, round2, halo_s, halo_r, halo_f, a2a_s, a2a_r, pag_s, pag_r, pfw_s, pfw_r,
+    oa_s, oa_r, oh_s, oh_r, c_s, c_r, xy_s, xy_r, z_s, z_r, f_s, f_r,
 ):
     p = lax.axis_index("pos")
     m = lax.axis_index("mode")
@@ -80,6 +80,22 @@
 
     def band(k):
         return pl.ds(pl.multiple_of(k * Q, Q), Q)
+
+    def signal(sem, targets):
+        for pos, mode in targets:
+            pl.semaphore_signal(sem, inc=1, device_id=(pos, mode), device_id_type=pl.DeviceIdType.MESH)
+
+    def z_plus(d):
+        return lax.rem(z + (d + NZ), NZ)
+
+    z_twin = z + 1 - 2 * lax.rem(z, 2)
+    x_partners = [(p, mode_plus(d)) for d in range(1, NX)]
+    y_partners = [(at(lax.rem(y + d, NY), z, c), m) for d in range(1, NY)]
+
+    near = [(pos_plus(d), m) for d in (5, 4, 1, -1, -4, -5)] + [(at(y, z_plus(d), c), m) for d in (2, -2)]
+    near += [(at(y, z_twin, c), m)] + x_partners + y_partners
+    barrier = pltpu.get_barrier_semaphore()
+    signal(barrier, near)
 
     mine = band(m)
     loads = [
@@ -88,25 +104,12 @@
         pltpu.make_async_copy(phase, ph, load_sem.at[2]),
         pltpu.make_async_copy(measured.at[m], meas, load_sem.at[3]),
         pltpu.make_async_copy(tables, tab, load_sem.at[4]),
+        pltpu.make_async_copy(corners, offs, load_sem.at[5]),
     ]
     for copy in loads:
         copy.start()
 
-    partners = []
-    for d in HALO:
-        partners += [(pos_plus(d), m), (pos_plus(-d), m)]
-    for dx in range(NX):
-        for dy in range(NY):
-            if dx or dy:
-                partners.append((at(lax.rem(y + dy, NY), z, c), mode_plus(dx)))
-    for d in range(1, NZ):
-        partners.append((at(y, lax.rem(z + d, NZ), c), m))
-    for dy in range(1, NY):
-        partners.append((at(lax.rem(y + dy, NY), z, 1 - c), m))
-    barrier = pltpu.get_barrier_semaphore()
-    for pos, mode in partners:
-        pl.semaphore_signal(barrier, inc=1, device_id=(pos, mode), device_id_type=pl.DeviceIdType.MESH)
-    pl.semaphore_wait(barrier, len(partners))
+    pl.semaphore_wait(barrier, len(near))
 
     started = []
 
@@ -115,27 +118,57 @@
         started.append(copy)
         return copy
 
-    halo = [[None] * 3 for _ in range(2)]
-    for s in range(2):
-        for h in (2, 1, 0):
-            halo[s][h] = go(remote(
-                tiles.at[0, s, :, mine, :], quarter.at[s, h + 1], halo_s.at[s, h], halo_r.at[s, h],
-                pos_plus(-HALO[h]), m,
-            ))
-        if s == 0:
-            pag = [
-                go(remote(probe.at[0, c], praw.at[m, c], pag_s.at[d - 1], pag_r.at[d - 1], p, mode_plus(d)))
-                for d in range(1, NX)
-            ]
+    col = lax.rem(p, COLS)
+    guarded = []
+
+    def guarded_go(cond, make):
+        @pl.when(cond)
+        def _():
+            make().start()
+
+        guarded.append((cond, make))
+
+    def halo_copy(s, h):
+        return remote(
+            tiles.at[0, s, :, mine, :], quarter.at[s, h + 1], halo_s.at[s, h], halo_r.at[s, h], pos_plus(-HALO[h]), m
+        )
+
+    def halo_forward(s):
+        return remote(
+            quarter.at[s, 2], quarter.at[s, 3], halo_f.at[s], halo_r.at[s, 2], at(y, z, 1 - c), m
+        )
+
+    def halo_send(s):
+        guarded_go(col == 2, lambda: halo_copy(s, 2))
+        go(halo_copy(s, 1))
+        guarded_go(col > 0, lambda: halo_copy(s, 0))
+
+    def halo_wait(s):
+        halo_copy(s, 1).wait_recv()
+        guarded_go(c == 1, lambda: halo_forward(s))
+
+        @pl.when(col < 3)
+        def _():
+            halo_copy(s, 0).wait_recv()
+            halo_copy(s, 2).wait_recv()
+
+    halo_send(0)
+    pag = [
+        go(remote(probe.at[0, c], praw.at[m, c], pag_s.at[d - 1], pag_r.at[d - 1], p, mode_plus(d)))
+        for d in range(1, NX)
+    ]
+    halo_send(1)
+    signal(round1, x_partners + [(at(y, z, 1 - c), m)] + [(at(y, z_plus(d), c), m) for d in (2, -2)])
 
     base_row = p // COLS * S
-    base_col = lax.rem(p, COLS) * S
+    base_col = col * S
     iota_r = lax.broadcasted_iota(jnp.int32, (Q, S), 0) + m * Q
     iota_c = lax.broadcasted_iota(jnp.int32, (Q, S), 1)
 
     def corner(k):
-        return offs[k, 0] - base_row, offs[k, 1] - base_col
-
+        return offs[0, k] - base_row, offs[1, k] - base_col
+
+    loads[5].wait()
     row0, col0 = corner(m)
     row_back, col_back = lax.rem(S - row0, S), lax.rem(S - col0, S)
 
@@ -147,8 +180,7 @@
     a2a = [[None] * 3 for _ in range(2)]
 
     def window_bands(s):
-        for h in range(3):
-            halo[s][h].wait_recv()
+        halo_wait(s)
         for k in range(NX):
             r, cc = corner(k)
             for plane in range(2):
@@ -163,6 +195,8 @@
         win[s, :, mine, :] = rows_sel[s, m]
 
     window_bands(0)
+    pl.semaphore_wait(round1, 6)
+    signal(round2, [(at(y, z_twin, c), m)] + [(at(y, z_plus(d), c), m) for d in (4, -4)])
 
     loads[1].wait()
     pfw = []
@@ -245,8 +279,37 @@
     send_object(1)
 
     cc_copies = [None] * NX
+    half = lax.rem(z, 2)
+
+    def rows16(yy, zz):
+        return pl.ds(pl.multiple_of(yy * Q + zz * 16, 16), 16)
+
+    def send_probe(k):
+        cc_copies[k].wait_recv()
+        pg[k, c] = pg[k, c] + rxc[k]
+        dx = lax.rem(k - m + NX, NX)
+        for dz in range(2):
+            zz = half if dz == 0 else 1 - half
+            for dy in range(NY):
+                yy = lax.rem(y + dy, NY)
+
+                def make(dz=dz, dy=dy, zz=zz, yy=yy):
+                    return remote(
+                        pg.at[k, c, rows16(yy, zz), :], rxy.at[dx, dy, dz], xy_s.at[dx, dy, dz], xy_r.at[dx, dy, dz],
+                        at(yy, z if dz == 0 else z_twin, c), k,
+                    )
+
+                if dy or dz:
+                    go(make())
+                else:
+                    guarded_go(k != m, make)
+
     for index, pair in enumerate(pairs):
         spec = transform(*[cmul(both(win, 1), both(far, k)) for k in pair], False)
+        if index:
+            pl.semaphore_wait(round2, 3)
+            for k in pairs[0]:
+                send_probe(k)
         first = transform(*[cmul((hc[...], hs[...]), v) for v in spec], True)
         for k, v in zip(pair, first):
             put(far, k, v)
@@ -260,32 +323,8 @@
     for plane in range(2):
         obj[0, plane] = (terms[0][plane] + terms[1][plane]) + (terms[2][plane] + terms[3][plane])
     send_object(0)
-
-    guarded = []
-
-    def guarded_go(cond, make):
-        @pl.when(cond)
-        def _():
-            make().start()
-
-        guarded.append((cond, make))
-
-    for k in range(NX):
-        cc_copies[k].wait_recv()
-        pg[k, c] = pg[k, c] + rxc[k]
-        dx = lax.rem(k - m + NX, NX)
-        for dy in range(NY):
-            yy = lax.rem(y + dy, NY)
-
-            def make(k=k, dx=dx, dy=dy, yy=yy):
-                return remote(
-                    pg.at[k, c, band(yy), :], rxy.at[dx, dy], xy_s.at[dx, dy], xy_r.at[dx, dy], at(yy, z, c), k,
-                )
-
-            if dy:
-                go(make())
-            else:
-                guarded_go(k != m, make)
+    for k in pairs[1]:
+        send_probe(k)
 
     oh = [[None] * 3 for _ in range(2)]
 
@@ -312,76 +351,77 @@
             for h in range(3):
                 hsend[s, h, plane] = sums[h + 1][plane]
         for h in (2, 1, 0):
-            oh[s][h] = go(remote(
-                hsend.at[s, h], hrecv.at[s, h], oh_s.at[s, h], oh_r.at[s, h], pos_plus(HALO[h]), m,
-            ))
+            def make(h=h):
+                return remote(
+                    hsend.at[s, h], hrecv.at[s, h], oh_s.at[s, h], oh_r.at[s, h], pos_plus(HALO[h]), m,
+                )
+
+            oh[s][h] = make()
+            if h == 1:
+                go(make())
+            else:
+                guarded_go(col < 3, make)
 
     spread_object(1)
     spread_object(0)
 
-    def wait_recv_xy(dx, dy):
-        remote(rxy.at[dx, dy], rxy.at[dx, dy], xy_s.at[dx, dy], xy_r.at[dx, dy], p, m).wait_recv()
-
-    part = pg[m, c, band(y), :]
+    part = pg[m, c, rows16(y, half), :]
     for dx in range(NX):
         for dy in range(NY):
-            if dx or dy:
-                wait_recv_xy(dx, dy)
-                part = part + rxy[dx, dy]
-    for i in range(4):
-        zs[i] = part[8 * i : 8 * i + 8]
-
-    owner = lax.rem(z, 4) == 0
-    own = z // 4
-    for i in range(4):
-        d = lax.rem(4 * i - z + NZ, NZ)
-
-        def make(i=i, d=d):
-            return remote(zs.at[i], rxz.at[d], z_s.at[i], z_r.at[d], at(y, 4 * i, c), m)
-
-        guarded_go(z != 4 * i, make)
-
-    def z_gather(d):
-        return remote(gz.at[own], gz.at[own], zg_s.at[d], zg_r.at[own], at(y, lax.rem(z + d, NZ), c), m)
-
-    @pl.when(owner)
+            for dz in range(2):
+                if dx or dy or dz:
+                    slot = rxy.at[dx, dy, dz]
+                    remote(slot, slot, xy_s.at[dx, dy, dz], xy_r.at[dx, dy, dz], *x_partners[0]).wait_recv()
+                    part = part + rxy[dx, dy, dz]
+
+    place = z // 2
+    zs[place] = part
+    far_z = []
+    for d in range(1, NZ // 2):
+        far_z.append(go(remote(
+            zs.at[place], zs.at[place], z_s.at[d], z_r.at[d], at(y, z_plus(2 * d), c), m,
+        )))
+    for copy in far_z:
+        copy.wait_recv()
+    full = zs[0]
+    for i in range(1, NZ // 2):
+        full = full + zs[i]
+    pgall[c, y, half] = full * (1.0 / math.sqrt(NX * NP))
+
+    last = []
+    for dz in range(2):
+        for dy in range(NY):
+            for dc in range(NC):
+                if dc or dy or dz:
+                    own = pgall.at[c, y, half]
+                    last.append(go(remote(
+                        own, own, f_s.at[dc, dy, dz], f_r.at[dc, dy, dz],
+                        at(lax.rem(y + dy, NY), z_twin if dz else z, 1 - c if dc else c), m,
+                    )))
+
+    @pl.when(col == 0)
     def _():
-        full = zs[own]
-        for d in range(1, NZ):
-            remote(rxz.at[d], rxz.at[d], z_s.at[0], z_r.at[d], p, m).wait_recv()
-            full = full + rxz[d]
-        gz[own] = full * (1.0 / math.sqrt(NX * NP))
-        for d in range(1, NZ):
-            z_gather(d).start()
+        for s in range(2):
+            for h in (0, 2):
+                hrecv[s, h] = jnp.zeros_like(hrecv[s, h])
+
+    @pl.when(col > 0)
+    def _():
+        for s in range(2):
+            for h in (0, 2):
+                oh[s][h].wait_recv()
 
     for s in range(2):
-        for h in range(3):
-            oh[s][h].wait_recv()
+        oh[s][1].wait_recv()
         for plane in range(2):
             out_obj[0, s, plane] = (hown[s, plane] + hrecv[s, 0, plane]) + (hrecv[s, 1, plane] + hrecv[s, 2, plane])
 
-    for i in range(4):
-        @pl.when(z != 4 * i)
-        def _(i=i):
-            remote(gz.at[i], gz.at[i], zg_s.at[0], zg_r.at[i], p, m).wait_recv()
-
-    for i in range(4):
-        pgall[c, y, i] = gz[i]
-    last = []
-    for dc in range(NC):
-        for dy in range(NY):
-            if dc or dy:
-                yy = lax.rem(y + dy, NY)
-                cc = lax.rem(c + dc, NC)
-                last.append(go(remote(
-                    gz, pgall.at[c, y], f_s.at[dc, dy], f_r.at[dc, dy], at(yy, z, cc), m,
-                )))
     for copy in last:
         copy.wait_recv()
     for plane in range(2):
         for yy in range(NY):
-            for i in range(4):
-                out_probe[0, plane, yy * Q + 8 * i : yy * Q + 8 * i + 8] = pgall[plane, yy, i]
+            for i in range(2):
+                out_probe[0, plane, yy * Q + 16 * i : yy * Q + 16 * i + 16] = pgall[plane, yy, i]
 
     for copy in started:
         copy.wait_send()
@@ -389,11 +429,6 @@
         @pl.when(cond)
         def _(make=make):
             make().wait_send()
-
-    @pl.when(owner)
-    def _():
-        for d in range(1, NZ):
-            z_gather(d).wait_send()
 
 
 def body(tables, tiles, probe, phase, offs, measured):
@@ -406,9 +441,10 @@
             jax.ShapeDtypeStruct((1, 2, 2, Q, S), F32),
             jax.ShapeDtypeStruct((1, 2, S, S), F32),
         ),
-        in_specs=[any_space, any_space, any_space, pl.BlockSpec(memory_space=pltpu.SMEM), any_space, any_space],
+        in_specs=[any_space] * 6,
         out_specs=(pl.BlockSpec(memory_space=vmem), pl.BlockSpec(memory_space=vmem)),
         scratch_shapes=[
+            pltpu.SMEM((2, NX), jnp.int32),
             vmem((2, 4, 2, Q, S), F32),
             vmem((2, NX, 2, Q, S), F32),
             vmem((2, 2, S, S), F32),
@@ -428,23 +464,20 @@
             vmem((2, 3, 2, Q, S), F32),
             vmem((NX, 2, S, S), F32),
             vmem((NX, S, S), F32),
-            vmem((NX, NY, Q, S), F32),
-            vmem((4, 8, S), F32),
-            vmem((NZ, 8, S), F32),
-            vmem((4, 8, S), F32),
-            vmem((NC, NY, 4, 8, S), F32),
-            dma((5,)),
-            dma((2, 3)), dma((2, 3)), dma((2, 3)), dma((2, 3)),
+            vmem((NX, NY, 2, 16, S), F32),
+            vmem((NZ // 2, 16, S), F32),
+            vmem((NC, NY, 2, 16, S), F32),
+            dma((6,)), pltpu.SemaphoreType.REGULAR, pltpu.SemaphoreType.REGULAR,
+            dma((2, 3)), dma((2, 3)), dma((2,)), dma((2, 3)), dma((2, 3)),
             dma((3,)), dma((3,)), dma((3,)), dma((3,)),
             dma((2, 3)), dma((2, 3)), dma((2, 3)), dma((2, 3)),
-            dma((NX,)), dma((NX,)), dma((NX, NY)), dma((NX, NY)),
-            dma((4,)), dma((NZ,)), dma((NZ,)), dma((4,)),
-            dma((NC, NY)), dma((NC, NY)),
+            dma((NX,)), dma((NX,)), dma((NX, NY, 2)), dma((NX, NY, 2)),
+            dma((NZ // 2,)), dma((NZ // 2,)), dma((NC, NY, 2)), dma((NC, NY, 2)),
         ],
         compiler_params=pltpu.CompilerParams(
-            collective_id=0, has_side_effects=True, vmem_limit_bytes=32 * 1024 * 1024
+            collective_id=0, has_side_effects=True, vmem_limit_bytes=24 * 1024 * 1024
         ),
-    )(tiles, probe, phase, offs, measured, tables)
+    )(*[pltpu.with_memory_space_constraint(v, pltpu.HBM) for v in (tiles, probe, phase, offs.T, measured, tables)])
 
 
 def solution(mesh):

time: 71.4 us -> 55.4 us (0.78)
  Pallas kernels: 63.8 us -> 53.3 us
  local copies, waits for them, and re-layouts: 6.74 us -> 1.29 us
    pallas_call x1, Pallas kernels: 63.8 us -> 53.3 us  [body(): pl.pallas_call(kernel, out_shape=(jax.ShapeDtypeStruct((1, 2, 2, Q, S), F...]
    unnamed x13 -> x2, local copies, waits for them, and re-layouts: 6.74 us -> 1.29 us
where the time goes in v2:
time: 55.4 us; the launch traced here: 55.3 us
  Pallas kernels  53.3 us (96%)
  local copies, waits for them, and re-layouts  1.29 us (2%)
  between operations  0.64 us (1%)
    pallas_call x1, Pallas kernels, body(): pl.pallas_call(kernel, out_shape=(jax.ShapeDtypeStruct((1, 2, 2, Q, S), F...  53.3 us
    unnamed x2, local copies, waits for them, and re-layouts  1.29 us

profile of v2, /device:TPU:1, one launch (start us, length us, event | category | flops | bytes accessed | tf_op | source)
XLA Modules:
  0.0 55.3 jit_solution(4048388892283690720)
XLA Ops:
  0.6 53.3 %shard_map.77 = (f32[1,2,2,32,128]{4,3,2,1,0:T(8,128)S(1)}, f32[1,2,128,128]{3,2,1,0:T(8,128)S(1)}) custom-call(f32[1,2,2,128,128]{4,3,2,1,0:T(8,128)} %tiles.1, f32[1,2,128,128]{3,2,1,0:T(8,128)} %probe.1, f32[128,128]{1,0:T(8,128)} %phase.1, s32[2,4]{1,0:T(2,128)} %bitcast.1, f32[4,128,128]{2,1,0:T(8,128)} %measured.1, ...), custom_call_target="tpu_custom_call" | custom-call | tf_op jit(solution)/shard_map/pallas_call | solution.py:438
  54.0 0.6 %copy.10 = f32[1,2,2,32,128]{4,3,2,1,0:T(8,128)} copy(f32[1,2,2,32,128]{4,3,2,1,0:T(8,128)S(1)} %get-tuple-element.4) | data formatting | bytes 131072
  54.6 0.7 %copy.11 = f32[1,2,128,128]{3,2,1,0:T(8,128)} copy(f32[1,2,128,128]{3,2,1,0:T(8,128)S(1)} %get-tuple-element.5) | data formatting | bytes 262144

commit v3 on v2

v3 whole, which is shorter than its diff:
```python
import math

import jax
import jax.numpy as jnp
from jax import lax
from jax.experimental import pallas as pl
from jax.experimental.pallas import tpu as pltpu
from jax.sharding import PartitionSpec as P

NX, NY, NZ, NC = 4, 4, 16, 2
NP = NY * NZ * NC
COLS = 4
S = 128
Q = S // NX
F32 = jnp.float32
BF16 = jnp.bfloat16
CUT = 2
HALO = (1, COLS, COLS + 1)


def split(x):
    hi = x.astype(BF16)
    return hi, (x - hi.astype(F32)).astype(BF16)


def dot(a, b):
    return jnp.dot(a, b, preferred_element_type=F32)


def mul(a, b):
    return a[0] * b[0] - a[1] * b[1], a[0] * b[1] + a[1] * b[0]


def cmul(a, b):
    return a[0] * b[0] + a[1] * b[1], a[0] * b[1] - a[1] * b[0]


def kernel(
    tiles, probe, phase, corners, measured,
    out_obj, out_probe,
    offs, quarter, rows_sel, win, praw, prb, ph, hc, hs, meas, tab, psi, far, obj, rxo, hsend, hown, hrecv,
    pg, rxc, rxy, zs, pgall,
    load_sem, round1, round2, halo_s, below_r, side_r, a2a_s, a2a_r, pag_s, pag_r, pfw_s, pfw_r,
    oa_s, oa_r, oh_s, oh_r, c_s, c_r, xy_s, xy_r, z_s, z_r, f_s, f_r,
):
    p = lax.axis_index("pos")
    m = lax.axis_index("mode")
    c = lax.rem(p, NC)
    z = lax.rem(p // NC, NZ)
    y = p // (NC * NZ)

    def at(yy, zz, cc):
        return (yy * NZ + zz) * NC + cc

    def pos_plus(d):
        return lax.rem(p + (d + NP), NP)

    def mode_plus(d):
        return lax.rem(m + (d + NX), NX)

    def remote(src, dst, ss, rs, pos, mode):
        return pltpu.make_async_remote_copy(
            src_ref=src, dst_ref=dst, send_sem=ss, recv_sem=rs,
            device_id=(pos, mode), device_id_type=pl.DeviceIdType.MESH,
        )

    def arrived(ref, sem):
        remote(ref, ref, sem, sem, *x_partners[0]).wait_recv()

    def sent(ref, sem):
        remote(ref, ref, sem, sem, *x_partners[0]).wait_send()

    def band(k):
        return pl.ds(pl.multiple_of(k * Q, Q), Q)

    def signal(sem, targets):
        for pos, mode in targets:
            pl.semaphore_signal(sem, inc=1, device_id=(pos, mode), device_id_type=pl.DeviceIdType.MESH)

    def z_plus(d):
        return lax.rem(z + (d + NZ), NZ)

    z_twin = z + 1 - 2 * lax.rem(z, 2)
    x_partners = [(p, mode_plus(d)) for d in range(1, NX)]
    y_partners = [(at(lax.rem(y + d, NY), z, c), m) for d in range(1, NY)]

    near = [(pos_plus(d), m) for d in (5, 4, 1, -1, -4, -5)] + [(at(y, z_plus(d), c), m) for d in (2, -2)]
    near += [(at(y, z_twin, c), m)] + x_partners + y_partners
    barrier = pltpu.get_barrier_semaphore()
    signal(barrier, near)

    mine = band(m)
    loads = [
        pltpu.make_async_copy(tiles.at[0, :, :, mine, :], quarter.at[:, 0], load_sem.at[0]),
        pltpu.make_async_copy(probe.at[0], praw.at[m], load_sem.at[1]),
        pltpu.make_async_copy(phase, ph, load_sem.at[2]),
        pltpu.make_async_copy(measured.at[m], meas, load_sem.at[3]),
        pltpu.make_async_copy(corners, offs, load_sem.at[4]),
    ]
    for copy in loads:
        copy.start()

    pl.semaphore_wait(barrier, len(near))

    col = lax.rem(p, COLS)

    loads[0].wait()
    loads[1].wait()
    width = 2 // CUT
    pieces = [(s, pl.ds(i * width, width)) for s in range(2) for i in range(CUT)]

    def halo_send(s, planes):
        i = pieces.index((s, planes))
        for h in (2, 1, 0):
            def start(h=h):
                remote(
                    quarter.at[s, 0, planes], quarter.at[s, h + 1, planes], halo_s.at[h],
                    below_r.at[i] if h == 1 else side_r.at[i], pos_plus(-HALO[h]), m,
                ).start()

            if h == 1:
                start()
            else:
                pl.when(col == 2 if h == 2 else col > 0)(start)

    def halo_wait(s, planes):
        i = pieces.index((s, planes))
        arrived(quarter.at[s, 2, planes], below_r.at[i])

        @pl.when(c == 1)
        def _():
            remote(
                quarter.at[s, 2, planes], quarter.at[s, 3, planes], halo_s.at[3], side_r.at[i], at(y, z, 1 - c), m
            ).start()

        @pl.when(col < 3)
        def _():
            arrived(quarter.at[s, 0:2, planes], side_r.at[i])

    for piece in pieces[:CUT]:
        halo_send(*piece)
    for d in (2, 1, 3):
        remote(praw.at[m, c], praw.at[m, c], pag_s, pag_r, p, mode_plus(d)).start()
    for piece in pieces[CUT:]:
        halo_send(*piece)
    signal(round1, x_partners + [(at(y, z, 1 - c), m)] + [(at(y, z_plus(d), c), m) for d in (2, -2)])

    base_row = p // COLS * S
    base_col = col * S
    iota_r = lax.broadcasted_iota(jnp.int32, (Q, S), 0) + m * Q
    iota_c = lax.broadcasted_iota(jnp.int32, (Q, S), 1)

    def corner(k):
        return offs[0, k] - base_row, offs[1, k] - base_col

    loads[4].wait()
    row0, col0 = corner(m)
    row_back, col_back = lax.rem(S - row0, S), lax.rem(S - col0, S)

    index = lax.broadcasted_iota(jnp.int32, (S, S), 0) * lax.broadcasted_iota(jnp.int32, (S, S), 1)
    angle = lax.rem(index, S).astype(F32) * (2.0 * math.pi / S)
    cos_parts, sin_parts = split(jnp.cos(angle) * S**-0.5), split(jnp.sin(angle) * S**-0.5)
    for i in range(2):
        for t in range(2):
            tab[t, i, :S, :S] = cos_parts[i]
            tab[t, i, S:, S:] = cos_parts[i]
            tab[t, i, S * (1 - t) : S * (2 - t), S * t : S * (t + 1)] = sin_parts[i]
            tab[t, i, S * t : S * (t + 1), S * (1 - t) : S * (2 - t)] = -sin_parts[i]
    loads[2].wait()
    hc[...] = jnp.cos(ph[...])
    hs[...] = jnp.sin(ph[...])

    def window_bands(s, planes):
        halo_wait(s, planes)
        for k in range(NX):
            r, cc = corner(k)
            for plane in range(planes.start, planes.start + planes.size):
                upper = jnp.where(iota_c >= cc, quarter[s, 0, plane], quarter[s, 1, plane])
                lower = jnp.where(iota_c >= cc, quarter[s, 2, plane], quarter[s, 3, plane])
                rows_sel[s, k, plane] = jnp.where(iota_r >= r, upper, lower)
        for d in (2, 1, 3):
            k = mode_plus(d)
            remote(rows_sel.at[s, k, planes], win.at[s, planes, mine, :], a2a_s, a2a_r.at[s], p, k).start()
        win[s, planes, mine, :] = rows_sel[s, m, planes]

    def window_wait(s):
        arrived(win.at[s, :, pl.ds(0, S - Q), :], a2a_r.at[s])

    for piece in pieces[:CUT]:
        window_bands(*piece)
    pl.semaphore_wait(round1, 6)
    signal(round2, [(at(y, z_twin, c), m)] + [(at(y, z_plus(d), c), m) for d in (4, -4)])

    arrived(praw.at[0:3, 0], pag_r)
    for d in range(1, NX):
        k = mode_plus(-d)
        remote(praw.at[k, c], praw.at[k, c], pfw_s, pfw_r, at(y, z, 1 - c), m).start()
    for piece in pieces[CUT:]:
        window_bands(*piece)
    arrived(praw.at[0:3, 0], pfw_r)
    order = (2, 1, 3, 0)
    for k in range(NX):
        for plane in range(2):
            prb[k, plane] = pltpu.roll(pltpu.roll(praw[mode_plus(order[k]), plane], row0, 0), col0, 1)

    loads[3].wait()

    def transform(a, b, inverse):
        right, left = (1, 0) if inverse else (0, 1)
        x = jnp.concatenate([jnp.concatenate(a, axis=1), jnp.concatenate(b, axis=1)], axis=0)
        hi, lo = split(x)
        w_hi, w_lo = tab[right, 0], tab[right, 1]
        o = dot(hi, w_hi) + (dot(lo, w_hi) + dot(hi, w_lo))
        x = jnp.concatenate(
            [
                jnp.concatenate([o[:S, :S], o[S:, :S]], axis=1),
                jnp.concatenate([o[:S, S:], o[S:, S:]], axis=1),
            ],
            axis=0,
        )
        hi, lo = split(x)
        w_hi, w_lo = tab[left, 0], tab[left, 1]
        o = dot(w_hi, hi) + (dot(w_hi, lo) + dot(w_lo, hi))
        return (o[:S, :S], o[S:, :S]), (o[:S, S:], o[S:, S:])

    def both(ref, k):
        return ref[k, 0], ref[k, 1]

    def put(ref, k, value):
        ref[k, 0] = value[0]
        ref[k, 1] = value[1]

    pairs = ((0, 1), (2, 3))
    window_wait(0)
    for pair in pairs:
        spec = transform(*[mul(both(prb, k), both(win, 0)) for k in pair], False)
        wave = transform(*[mul(v, (hc[...], hs[...])) for v in spec], True)
        for k, v in zip(pair, wave):
            put(psi, k, v)
    window_wait(1)
    for pair in pairs:
        wave = transform(*[mul(both(psi, k), both(win, 1)) for k in pair], False)
        for k, v in zip(pair, wave):
            put(far, k, v)
    total = -meas[...]
    for k in range(NX):
        total = total + (far[k, 0] * far[k, 0] + far[k, 1] * far[k, 1])
    meas[...] = total
    for pair in pairs:
        grad = transform(*[(meas[...] * far[k, 0], meas[...] * far[k, 1]) for k in pair], True)
        for k, v in zip(pair, grad):
            put(far, k, v)

    def send_object(s):
        for d in (2, 1, 3):
            k = mode_plus(d)
            remote(obj.at[s, :, band(k), :], rxo.at[s, d - 1], oa_s, oa_r.at[s], p, k).start()

    terms = [cmul(both(psi, k), both(far, k)) for k in range(NX)]
    for plane in range(2):
        obj[1, plane] = (terms[0][plane] + terms[1][plane]) + (terms[2][plane] + terms[3][plane])
    send_object(1)

    half = lax.rem(z, 2)

    def rows16(yy, zz):
        return pl.ds(pl.multiple_of(yy * Q + zz * 16, 16), 16)

    def send_probe(index, pair):
        arrived(rxc.at[pair[0] : pair[1] + 1], c_r.at[index])
        for k in pair:
            pg[k, c] = pg[k, c] + rxc[k]
            dx = order[k]
            for dz in range(2):
                zz = half if dz == 0 else 1 - half
                for dy in range(NY):
                    if dx or dy or dz:
                        yy = lax.rem(y + dy, NY)
                        remote(
                            pg.at[k, c, rows16(yy, zz), :], rxy.at[(dx * NY + dy) * 2 + dz], xy_s, xy_r,
                            at(yy, z_twin if dz else z, c), mode_plus(dx),
                        ).start()

    for index, pair in enumerate(pairs):
        spec = transform(*[cmul(both(win, 1), both(far, k)) for k in pair], False)
        if index:
            pl.semaphore_wait(round2, 3)
            send_probe(0, pairs[0])
        first = transform(*[cmul((hc[...], hs[...]), v) for v in spec], True)
        for k, v in zip(pair, first):
            put(far, k, v)
            back = cmul(both(win, 0), v)
            for plane in range(2):
                pg[k, plane] = pltpu.roll(pltpu.roll(back[plane], row_back, 0), col_back, 1)
            remote(pg.at[k, 1 - c], rxc.at[k], c_s, c_r.at[index], at(y, z, 1 - c), m).start()
    terms = [cmul(both(prb, k), both(far, k)) for k in range(NX)]
    for plane in range(2):
        obj[0, plane] = (terms[0][plane] + terms[1][plane]) + (terms[2][plane] + terms[3][plane])
    send_object(0)
    send_probe(1, pairs[1])

    def spread_object(s):
        arrived(rxo.at[s], oa_r.at[s])
        sums = [[None, None] for _ in range(4)]
        for d in range(NX):
            r, cc = corner(mode_plus(-d))
            low, high = iota_r >= r, iota_c >= cc
            for plane in range(2):
                v = rxo[s, d - 1, plane] if d else obj[s, plane, mine, :]
                zero = jnp.zeros_like(v)
                upper, lower = jnp.where(low, v, zero), jnp.where(low, zero, v)
                parts = (
                    jnp.where(high, upper, zero), jnp.where(high, zero, upper),
                    jnp.where(high, lower, zero), jnp.where(high, zero, lower),
                )
                for i in range(4):
                    old = sums[i][plane]
                    sums[i][plane] = parts[i] if old is None else old + parts[i]
        for plane in range(2):
            hown[s, plane] = sums[0][plane]
            for h in range(3):
                hsend[s, h, plane] = sums[h + 1][plane]
        for h in (2, 1, 0):
            def start(h=h):
                remote(
                    hsend.at[s, h], hrecv.at[h, s], oh_s.at[h], oh_r.at[1 if h == 1 else 0], pos_plus(HALO[h]), m
                ).start()

            if h == 1:
                start()
            else:
                pl.when(col < 3)(start)

    spread_object(1)
    spread_object(0)

    part = pg[order.index(0), c, rows16(y, half), :]
    arrived(rxy.at[1:], xy_r)
    for i in range(1, 2 * NX * NY):
        part = part + rxy[i]

    place = z // 2
    zs[place] = part
    for d in (4, 3, 5, 2, 6, 1, 7):
        remote(zs.at[place], zs.at[place], z_s, z_r, at(y, z_plus(2 * d), c), m).start()
    arrived(zs.at[1:], z_r)
    full = zs[0]
    for i in range(1, NZ // 2):
        full = full + zs[i]
    pgall[c, y, half] = full * (1.0 / math.sqrt(NX * NP))

    own = pgall.at[c, y, half]
    for dy in (2, 1, 3, 0):
        for dz in range(2):
            for dc in range(NC):
                if dc or dy or dz:
                    remote(
                        own, own, f_s, f_r,
                        at(lax.rem(y + dy, NY), z_twin if dz else z, 1 - c if dc else c), m,
                    ).start()

    @pl.when(col == 0)
    def _():
        for h in (0, 2):
            hrecv[h] = jnp.zeros_like(hrecv[h])

    @pl.when(col > 0)
    def _():
        arrived(hrecv.at[0:2], oh_r.at[0])

    arrived(hrecv.at[1], oh_r.at[1])
    for s in range(2):
        for plane in range(2):
            out_obj[0, s, plane] = (hown[s, plane] + hrecv[0, s, plane]) + (hrecv[1, s, plane] + hrecv[2, s, plane])

    arrived(rxy.at[0:15], f_r)
    for plane in range(2):
        for yy in range(NY):
            for i in range(2):
                out_probe[0, plane, yy * Q + 16 * i : yy * Q + 16 * i + 16] = pgall[plane, yy, i]

    sent(quarter.at[:, 0], halo_s.at[1])
    pl.when(col > 0)(lambda: sent(quarter.at[:, 0], halo_s.at[0]))
    pl.when(col == 2)(lambda: sent(quarter.at[:, 0], halo_s.at[2]))
    pl.when(c == 1)(lambda: sent(quarter.at[:, 0], halo_s.at[3]))
    sent(praw.at[0:3, 0], pag_s)
    sent(praw.at[0:3, 0], pfw_s)
    sent(rows_sel.at[:, 0:3], a2a_s)
    sent(rxo, oa_s)
    sent(rxc, c_s)
    sent(hown, oh_s.at[1])

    @pl.when(col < 3)
    def _():
        sent(hown, oh_s.at[0])
        sent(hown, oh_s.at[2])

    sent(rxy.at[1:], xy_s)
    sent(zs.at[1:], z_s)
    sent(rxy.at[0:15], f_s)


def body(tiles, probe, phase, offs, measured):
    any_space = pl.BlockSpec(memory_space=pl.ANY)
    vmem = pltpu.VMEM
    dma = pltpu.SemaphoreType.DMA
    return pl.pallas_call(
        kernel,
        out_shape=(
            jax.ShapeDtypeStruct((1, 2, 2, Q, S), F32),
            jax.ShapeDtypeStruct((1, 2, S, S), F32),
        ),
        in_specs=[any_space] * 5,
        out_specs=(pl.BlockSpec(memory_space=vmem), pl.BlockSpec(memory_space=vmem)),
        scratch_shapes=[
            pltpu.SMEM((2, NX), jnp.int32),
            vmem((2, 4, 2, Q, S), F32),
            vmem((2, NX, 2, Q, S), F32),
            vmem((2, 2, S, S), F32),
            vmem((NX, 2, S, S), F32),
            vmem((NX, 2, S, S), F32),
            vmem((S, S), F32),
            vmem((S, S), F32),
            vmem((S, S), F32),
            vmem((S, S), F32),
            vmem((2, 2, 2 * S, 2 * S), BF16),
            vmem((NX, 2, S, S), F32),
            vmem((NX, 2, S, S), F32),
            vmem((2, 2, S, S), F32),
            vmem((2, 3, 2, Q, S), F32),
            vmem((2, 3, 2, Q, S), F32),
            vmem((2, 2, Q, S), F32),
            vmem((3, 2, 2, Q, S), F32),
            vmem((NX, 2, S, S), F32),
            vmem((NX, S, S), F32),
            vmem((2 * NX * NY, 16, S), F32),
            vmem((NZ // 2, 16, S), F32),
            vmem((NC, NY, 2, 16, S), F32),
            dma((5,)), pltpu.SemaphoreType.REGULAR, pltpu.SemaphoreType.REGULAR,
            dma((4,)), dma((2 * CUT,)), dma((2 * CUT,)), dma, dma((2,)), dma, dma, dma, dma,
            dma, dma((2,)), dma((3,)), dma((2,)), dma, dma((2,)),
            dma, dma, dma, dma, dma, dma,
        ],
        compiler_params=pltpu.CompilerParams(
            collective_id=0, has_side_effects=True, vmem_limit_bytes=24 * 1024 * 1024
        ),
    )(*[pltpu.with_memory_space_constraint(v, pltpu.HBM) for v in (tiles, probe, phase, offs.T, measured)])


def solution(mesh):
    def run(tiles, probe, phase, offs, measured):
        return jax.shard_map(
            body,
            mesh=mesh,
            in_specs=(
                P("pos", None, None, None, None),
                P("mode", None, None, None),
                P(),
                P("pos", None),
                P("pos", None, None),
            ),
            out_specs=(P("pos", None, None, "mode", None), P("mode", None, None, None)),
            check_vma=False,
        )(tiles, probe, phase, offs, measured)

    return run
```

time: 55.4 us -> 53 us (0.957)
  Pallas kernels: 53.3 us -> 51 us
    pallas_call x1, Pallas kernels: 53.3 us -> 51 us  [body(): pl.pallas_call(kernel, out_shape=(jax.ShapeDtypeStruct((1, 2, 2, Q, S), F...]
where the time goes in v3:
time: 53 us; the launch traced here: 52.9 us
  Pallas kernels  51 us (96%)
  local copies, waits for them, and re-layouts  1.29 us (2%)
  between operations  0.64 us (1%)
    pallas_call x1, Pallas kernels, body(): pl.pallas_call(kernel, out_shape=(jax.ShapeDtypeStruct((1, 2, 2, Q, S), F...  51 us
    unnamed x2, local copies, waits for them, and re-layouts  1.29 us

profile of v3, /device:TPU:1, one launch (start us, length us, event | category | flops | bytes accessed | tf_op | source)
XLA Modules:
  0.0 52.9 jit_solution(8944819104297768855)
XLA Ops:
  0.6 51.0 %shard_map.68 = (f32[1,2,2,32,128]{4,3,2,1,0:T(8,128)S(1)}, f32[1,2,128,128]{3,2,1,0:T(8,128)S(1)}) custom-call(f32[1,2,2,128,128]{4,3,2,1,0:T(8,128)} %tiles.1, f32[1,2,128,128]{3,2,1,0:T(8,128)} %probe.1, f32[128,128]{1,0:T(8,128)} %phase.1, s32[2,4]{1,0:T(2,128)} %bitcast.1, f32[4,128,128]{2,1,0:T(8,128)} %measured.1), custom_call_target="tpu_custom_call" | custom-call | tf_op jit(solution)/shard_map/pallas_call | solution.py:407
  51.6 0.6 %copy.9 = f32[1,2,2,32,128]{4,3,2,1,0:T(8,128)} copy(f32[1,2,2,32,128]{4,3,2,1,0:T(8,128)S(1)} %get-tuple-element.4) | data formatting | bytes 131072
  52.2 0.7 %copy.10 = f32[1,2,128,128]{3,2,1,0:T(8,128)} copy(f32[1,2,128,128]{3,2,1,0:T(8,128)S(1)} %get-tuple-element.5) | data formatting | bytes 262144

commit v4 on v3

--- a/solution.py
+++ b/solution.py
@@ -38,10 +38,10 @@
 def kernel(
     tiles, probe, phase, corners, measured,
     out_obj, out_probe,
-    offs, quarter, rows_sel, win, praw, prb, ph, hc, hs, meas, tab, psi, far, obj, rxo, hsend, hown, hrecv,
+    offs, quarter, rows_sel, win, praw, prb, ph, hc, hs, meas, tab, psi, far, obj, rxo, hside, hown, hbelow, hside_in, hbelow_in,
     pg, rxc, rxy, zs, pgall,
     load_sem, round1, round2, halo_s, below_r, side_r, a2a_s, a2a_r, pag_s, pag_r, pfw_s, pfw_r,
-    oa_s, oa_r, oh_s, oh_r, c_s, c_r, xy_s, xy_r, z_s, z_r, f_s, f_r,
+    oa_s, oa_r, hs_s, hs_r, hb_s, hb_r, c_s, c_r, xy_s, xy_r, z_s, z_r, f_s, f_r,
 ):
     p = lax.axis_index("pos")
     m = lax.axis_index("mode")
@@ -88,6 +88,12 @@
     near += [(at(y, z_twin, c), m)] + x_partners + y_partners
     barrier = pltpu.get_barrier_semaphore()
     signal(barrier, near)
+
+    col = lax.rem(p, COLS)
+
+    @pl.when(col == 0)
+    def _():
+        hside_in[...] = jnp.zeros_like(hside_in)
 
     mine = band(m)
     loads = [
@@ -102,7 +108,6 @@
 
     pl.semaphore_wait(barrier, len(near))
 
-    col = lax.rem(p, COLS)
 
     loads[0].wait()
     loads[1].wait()
@@ -205,23 +210,25 @@
 
     loads[3].wait()
 
-    def transform(a, b, inverse):
+    def transform(groups, inverse):
         right, left = (1, 0) if inverse else (0, 1)
-        x = jnp.concatenate([jnp.concatenate(a, axis=1), jnp.concatenate(b, axis=1)], axis=0)
-        hi, lo = split(x)
-        w_hi, w_lo = tab[right, 0], tab[right, 1]
-        o = dot(hi, w_hi) + (dot(lo, w_hi) + dot(hi, w_lo))
-        x = jnp.concatenate(
-            [
-                jnp.concatenate([o[:S, :S], o[S:, :S]], axis=1),
-                jnp.concatenate([o[:S, S:], o[S:, S:]], axis=1),
-            ],
-            axis=0,
-        )
-        hi, lo = split(x)
-        w_hi, w_lo = tab[left, 0], tab[left, 1]
-        o = dot(w_hi, hi) + (dot(w_hi, lo) + dot(w_lo, hi))
-        return (o[:S, :S], o[S:, :S]), (o[:S, S:], o[S:, S:])
+        parts = []
+        for a, b in groups:
+            x = jnp.concatenate([jnp.concatenate(a, axis=1), jnp.concatenate(b, axis=1)], axis=0)
+            parts.append(split(x))
+        outs = [dot(hi, tab[right, 0]) + (dot(lo, tab[right, 0]) + dot(hi, tab[right, 1])) for hi, lo in parts]
+        parts = []
+        for o in outs:
+            x = jnp.concatenate(
+                [
+                    jnp.concatenate([o[:S, :S], o[S:, :S]], axis=1),
+                    jnp.concatenate([o[:S, S:], o[S:, S:]], axis=1),
+                ],
+                axis=0,
+            )
+            parts.append(split(x))
+        outs = [dot(tab[left, 0], hi) + (dot(tab[left, 0], lo) + dot(tab[left, 1], hi)) for hi, lo in parts]
+        return [((o[:S, :S], o[S:, :S]), (o[:S, S:], o[S:, S:])) for o in outs]
 
     def both(ref, k):
         return ref[k, 0], ref[k, 1]
@@ -232,22 +239,22 @@
 
     pairs = ((0, 1), (2, 3))
     window_wait(0)
-    for pair in pairs:
-        spec = transform(*[mul(both(prb, k), both(win, 0)) for k in pair], False)
-        wave = transform(*[mul(v, (hc[...], hs[...])) for v in spec], True)
+    specs = transform([[mul(both(prb, k), both(win, 0)) for k in pair] for pair in pairs], False)
+    waves = transform([[mul(v, (hc[...], hs[...])) for v in spec] for spec in specs], True)
+    for pair, wave in zip(pairs, waves):
         for k, v in zip(pair, wave):
             put(psi, k, v)
     window_wait(1)
-    for pair in pairs:
-        wave = transform(*[mul(both(psi, k), both(win, 1)) for k in pair], False)
+    waves = transform([[mul(both(psi, k), both(win, 1)) for k in pair] for pair in pairs], False)
+    for pair, wave in zip(pairs, waves):
         for k, v in zip(pair, wave):
             put(far, k, v)
     total = -meas[...]
     for k in range(NX):
         total = total + (far[k, 0] * far[k, 0] + far[k, 1] * far[k, 1])
     meas[...] = total
-    for pair in pairs:
-        grad = transform(*[(meas[...] * far[k, 0], meas[...] * far[k, 1]) for k in pair], True)
+    grads = transform([[(meas[...] * far[k, 0], meas[...] * far[k, 1]) for k in pair] for pair in pairs], True)
+    for pair, grad in zip(pairs, grads):
         for k, v in zip(pair, grad):
             put(far, k, v)
 
@@ -271,9 +278,9 @@
         for k in pair:
             pg[k, c] = pg[k, c] + rxc[k]
             dx = order[k]
-            for dz in range(2):
+            for dz in (1, 0):
                 zz = half if dz == 0 else 1 - half
-                for dy in range(NY):
+                for dy in (2, 1, 3, 0):
                     if dx or dy or dz:
                         yy = lax.rem(y + dy, NY)
                         remote(
@@ -281,23 +288,23 @@
                             at(yy, z_twin if dz else z, c), mode_plus(dx),
                         ).start()
 
+    specs = transform([[cmul(both(win, 1), both(far, k)) for k in pair] for pair in pairs], False)
+    firsts = transform([[cmul((hc[...], hs[...]), v) for v in spec] for spec in specs], True)
     for index, pair in enumerate(pairs):
-        spec = transform(*[cmul(both(win, 1), both(far, k)) for k in pair], False)
-        if index:
-            pl.semaphore_wait(round2, 3)
-            send_probe(0, pairs[0])
-        first = transform(*[cmul((hc[...], hs[...]), v) for v in spec], True)
+        first = firsts[index]
         for k, v in zip(pair, first):
             put(far, k, v)
             back = cmul(both(win, 0), v)
             for plane in range(2):
                 pg[k, plane] = pltpu.roll(pltpu.roll(back[plane], row_back, 0), col_back, 1)
             remote(pg.at[k, 1 - c], rxc.at[k], c_s, c_r.at[index], at(y, z, 1 - c), m).start()
+    pl.semaphore_wait(round2, 3)
+    send_probe(0, pairs[0])
+    send_probe(1, pairs[1])
     terms = [cmul(both(prb, k), both(far, k)) for k in range(NX)]
     for plane in range(2):
         obj[0, plane] = (terms[0][plane] + terms[1][plane]) + (terms[2][plane] + terms[3][plane])
     send_object(0)
-    send_probe(1, pairs[1])
 
     def spread_object(s):
         arrived(rxo.at[s], oa_r.at[s])
@@ -318,21 +325,24 @@
                     sums[i][plane] = parts[i] if old is None else old + parts[i]
         for plane in range(2):
             hown[s, plane] = sums[0][plane]
-            for h in range(3):
-                hsend[s, h, plane] = sums[h + 1][plane]
-        for h in (2, 1, 0):
-            def start(h=h):
-                remote(
-                    hsend.at[s, h], hrecv.at[h, s], oh_s.at[h], oh_r.at[1 if h == 1 else 0], pos_plus(HALO[h]), m
-                ).start()
-
-            if h == 1:
-                start()
-            else:
-                pl.when(col < 3)(start)
+            hbelow[s, plane] = sums[2][plane]
+            hside[s, 0, plane] = sums[1][plane]
+            hside[s, 1, plane] = sums[3][plane]
+
+        @pl.when(col < 3)
+        def _():
+            remote(hside.at[s], hside_in.at[s], hs_s, hs_r.at[s], pos_plus(1), m).start()
+
+    def send_below(s):
+        @pl.when(col > 0)
+        def _():
+            arrived(hside_in.at[s], hs_r.at[s])
+
+        for plane in range(2):
+            hbelow[s, plane] = hbelow[s, plane] + hside_in[s, 1, plane]
+        remote(hbelow.at[s], hbelow_in.at[s], hb_s, hb_r, pos_plus(COLS), m).start()
 
     spread_object(1)
-    spread_object(0)
 
     part = pg[order.index(0), c, rows16(y, half), :]
     arrived(rxy.at[1:], xy_r)
@@ -343,6 +353,9 @@
     zs[place] = part
     for d in (4, 3, 5, 2, 6, 1, 7):
         remote(zs.at[place], zs.at[place], z_s, z_r, at(y, z_plus(2 * d), c), m).start()
+    send_below(1)
+    spread_object(0)
+    send_below(0)
     arrived(zs.at[1:], z_r)
     full = zs[0]
     for i in range(1, NZ // 2):
@@ -359,19 +372,10 @@
                         at(lax.rem(y + dy, NY), z_twin if dz else z, 1 - c if dc else c), m,
                     ).start()
 
-    @pl.when(col == 0)
-    def _():
-        for h in (0, 2):
-            hrecv[h] = jnp.zeros_like(hrecv[h])
-
-    @pl.when(col > 0)
-    def _():
-        arrived(hrecv.at[0:2], oh_r.at[0])
-
-    arrived(hrecv.at[1], oh_r.at[1])
+    arrived(hbelow_in, hb_r)
     for s in range(2):
         for plane in range(2):
-            out_obj[0, s, plane] = (hown[s, plane] + hrecv[0, s, plane]) + (hrecv[1, s, plane] + hrecv[2, s, plane])
+            out_obj[0, s, plane] = hown[s, plane] + hside_in[s, 0, plane] + hbelow_in[s, plane]
 
     arrived(rxy.at[0:15], f_r)
     for plane in range(2):
@@ -388,13 +392,8 @@
     sent(rows_sel.at[:, 0:3], a2a_s)
     sent(rxo, oa_s)
     sent(rxc, c_s)
-    sent(hown, oh_s.at[1])
-
-    @pl.when(col < 3)
-    def _():
-        sent(hown, oh_s.at[0])
-        sent(hown, oh_s.at[2])
-
+    sent(hbelow, hb_s)
+    pl.when(col < 3)(lambda: sent(hside, hs_s))
     sent(rxy.at[1:], xy_s)
     sent(zs.at[1:], z_s)
     sent(rxy.at[0:15], f_s)
@@ -428,9 +427,11 @@
             vmem((NX, 2, S, S), F32),
             vmem((2, 2, S, S), F32),
             vmem((2, 3, 2, Q, S), F32),
-            vmem((2, 3, 2, Q, S), F32),
+            vmem((2, 2, 2, Q, S), F32),
             vmem((2, 2, Q, S), F32),
-            vmem((3, 2, 2, Q, S), F32),
+            vmem((2, 2, Q, S), F32),
+            vmem((2, 2, 2, Q, S), F32),
+            vmem((2, 2, Q, S), F32),
             vmem((NX, 2, S, S), F32),
             vmem((NX, S, S), F32),
             vmem((2 * NX * NY, 16, S), F32),
@@ -438,7 +439,7 @@
             vmem((NC, NY, 2, 16, S), F32),
             dma((5,)), pltpu.SemaphoreType.REGULAR, pltpu.SemaphoreType.REGULAR,
             dma((4,)), dma((2 * CUT,)), dma((2 * CUT,)), dma, dma((2,)), dma, dma, dma, dma,
-            dma, dma((2,)), dma((3,)), dma((2,)), dma, dma((2,)),
+            dma, dma((2,)), dma, dma((2,)), dma, dma, dma, dma((2,)),
             dma, dma, dma, dma, dma, dma,
         ],
         compiler_params=pltpu.CompilerParams(

time: 53 us -> 48.8 us (0.921)
  Pallas kernels: 51 us -> 46.7 us
    pallas_call x1, Pallas kernels: 51 us -> 46.7 us  [body(): pl.pallas_call(kernel, out_shape=(jax.ShapeDtypeStruct((1, 2, 2, Q, S), F...]
where the time goes in v4:
time: 48.8 us; the launch traced here: 48.7 us
  Pallas kernels  46.7 us (96%)
  local copies, waits for them, and re-layouts  1.29 us (3%)
  between operations  0.64 us (1%)
    pallas_call x1, Pallas kernels, body(): pl.pallas_call(kernel, out_shape=(jax.ShapeDtypeStruct((1, 2, 2, Q, S), F...  46.7 us
    unnamed x2, local copies, waits for them, and re-layouts  1.29 us

profile of v4, /device:TPU:1, one launch (start us, length us, event | category | flops | bytes accessed | tf_op | source)
XLA Modules:
  0.0 48.7 jit_solution(515504340394295267)
XLA Ops:
  0.6 46.7 %shard_map.68 = (f32[1,2,2,32,128]{4,3,2,1,0:T(8,128)S(1)}, f32[1,2,128,128]{3,2,1,0:T(8,128)S(1)}) custom-call(f32[1,2,2,128,128]{4,3,2,1,0:T(8,128)} %tiles.1, f32[1,2,128,128]{3,2,1,0:T(8,128)} %probe.1, f32[128,128]{1,0:T(8,128)} %phase.1, s32[2,4]{1,0:T(2,128)} %bitcast.1, f32[4,128,128]{2,1,0:T(8,128)} %measured.1), custom_call_target="tpu_custom_call" | custom-call | tf_op jit(solution)/shard_map/pallas_call | solution.py:406
  47.4 0.6 %copy.9 = f32[1,2,2,32,128]{4,3,2,1,0:T(8,128)} copy(f32[1,2,2,32,128]{4,3,2,1,0:T(8,128)S(1)} %get-tuple-element.4) | data formatting | bytes 131072
  48.0 0.7 %copy.10 = f32[1,2,128,128]{3,2,1,0:T(8,128)} copy(f32[1,2,128,128]{3,2,1,0:T(8,128)S(1)} %get-tuple-element.5) | data formatting | bytes 262144

commit v5 on v4

--- a/solution.py
+++ b/solution.py
@@ -212,23 +212,23 @@
 
     def transform(groups, inverse):
         right, left = (1, 0) if inverse else (0, 1)
-        parts = []
-        for a, b in groups:
-            x = jnp.concatenate([jnp.concatenate(a, axis=1), jnp.concatenate(b, axis=1)], axis=0)
-            parts.append(split(x))
-        outs = [dot(hi, tab[right, 0]) + (dot(lo, tab[right, 0]) + dot(hi, tab[right, 1])) for hi, lo in parts]
-        parts = []
-        for o in outs:
-            x = jnp.concatenate(
-                [
-                    jnp.concatenate([o[:S, :S], o[S:, :S]], axis=1),
-                    jnp.concatenate([o[:S, S:], o[S:, S:]], axis=1),
-                ],
-                axis=0,
-            )
-            parts.append(split(x))
-        outs = [dot(tab[left, 0], hi) + (dot(tab[left, 0], lo) + dot(tab[left, 1], hi)) for hi, lo in parts]
-        return [((o[:S, :S], o[S:, :S]), (o[:S, S:], o[S:, S:])) for o in outs]
+
+        def first(wave):
+            hi, lo = split(jnp.concatenate(wave, axis=1))
+            return dot(hi, tab[right, 0]) + (dot(lo, tab[right, 0]) + dot(hi, tab[right, 1]))
+
+        def second(o):
+            hi, lo = split(jnp.concatenate(
+                [jnp.concatenate([v[:, part * S : (part + 1) * S] for v in o], axis=1) for part in range(2)], axis=0
+            ))
+            u = []
+            for part in range(2):
+                rows = slice(part * S, (part + 1) * S)
+                u.append(dot(tab[left, 0, rows], hi) + (dot(tab[left, 0, rows], lo) + dot(tab[left, 1, rows], hi)))
+            return (u[0][:, :S], u[1][:, :S]), (u[0][:, S:], u[1][:, S:])
+
+        outs = [[first(wave) for wave in group] for group in groups]
+        return [second(o) for o in outs]
 
     def both(ref, k):
         return ref[k, 0], ref[k, 1]

time: 48.8 us -> 48.2 us (0.988)
  Pallas kernels: 46.7 us -> 46.1 us
    pallas_call x1, Pallas kernels: 46.7 us -> 46.1 us  [body(): pl.pallas_call(kernel, out_shape=(jax.ShapeDtypeStruct((1, 2, 2, Q, S), F...]
where the time goes in v5:
time: 48.2 us; the launch traced here: 48.1 us
  Pallas kernels  46.1 us (96%)
  local copies, waits for them, and re-layouts  1.29 us (3%)
  between operations  0.64 us (1%)
    pallas_call x1, Pallas kernels, body(): pl.pallas_call(kernel, out_shape=(jax.ShapeDtypeStruct((1, 2, 2, Q, S), F...  46.1 us
    unnamed x2, local copies, waits for them, and re-layouts  1.29 us

profile of v5, /device:TPU:1, one launch (start us, length us, event | category | flops | bytes accessed | tf_op | source)
XLA Modules:
  0.0 48.1 jit_solution(17295420979223751708)
XLA Ops:
  0.6 46.1 %shard_map.68 = (f32[1,2,2,32,128]{4,3,2,1,0:T(8,128)S(1)}, f32[1,2,128,128]{3,2,1,0:T(8,128)S(1)}) custom-call(f32[1,2,2,128,128]{4,3,2,1,0:T(8,128)} %tiles.1, f32[1,2,128,128]{3,2,1,0:T(8,128)} %probe.1, f32[128,128]{1,0:T(8,128)} %phase.1, s32[2,4]{1,0:T(2,128)} %bitcast.1, f32[4,128,128]{2,1,0:T(8,128)} %measured.1), custom_call_target="tpu_custom_call" | custom-call | tf_op jit(solution)/shard_map/pallas_call | solution.py:406
  46.8 0.6 %copy.9 = f32[1,2,2,32,128]{4,3,2,1,0:T(8,128)} copy(f32[1,2,2,32,128]{4,3,2,1,0:T(8,128)S(1)} %get-tuple-element.4) | data formatting | bytes 131072
  47.4 0.7 %copy.10 = f32[1,2,128,128]{3,2,1,0:T(8,128)} copy(f32[1,2,128,128]{3,2,1,0:T(8,128)S(1)} %get-tuple-element.5) | data formatting | bytes 262144

commit v6 on v5

--- a/solution.py
+++ b/solution.py
@@ -33,6 +33,12 @@
 
 def cmul(a, b):
     return a[0] * b[0] + a[1] * b[1], a[0] * b[1] - a[1] * b[0]
+
+
+def tree_sum(values):
+    while len(values) > 1:
+        values = [sum(values[i + 1 : i + 2], values[i]) for i in range(0, len(values), 2)]
+    return values[0]
 
 
 def kernel(
@@ -346,8 +352,7 @@
 
     part = pg[order.index(0), c, rows16(y, half), :]
     arrived(rxy.at[1:], xy_r)
-    for i in range(1, 2 * NX * NY):
-        part = part + rxy[i]
+    part = tree_sum([part] + [rxy[i] for i in range(1, 2 * NX * NY)])
 
     place = z // 2
     zs[place] = part
@@ -357,9 +362,7 @@
     spread_object(0)
     send_below(0)
     arrived(zs.at[1:], z_r)
-    full = zs[0]
-    for i in range(1, NZ // 2):
-        full = full + zs[i]
+    full = tree_sum([zs[i] for i in range(NZ // 2)])
     pgall[c, y, half] = full * (1.0 / math.sqrt(NX * NP))
 
     own = pgall.at[c, y, half]

time: 48.2 us -> 48.2 us (level)
  no operation moved by 1% of the time
where the time goes in v6:
time: 48.2 us; the launch traced here: 48 us
  Pallas kernels  46.1 us (96%)
  local copies, waits for them, and re-layouts  1.29 us (3%)
  between operations  0.64 us (1%)
    pallas_call x1, Pallas kernels, body(): pl.pallas_call(kernel, out_shape=(jax.ShapeDtypeStruct((1, 2, 2, Q, S), F...  46.1 us
    unnamed x2, local copies, waits for them, and re-layouts  1.29 us

profile of v6, /device:TPU:1, one launch (start us, length us, event | category | flops | bytes accessed | tf_op | source)
XLA Modules:
  0.0 48.0 jit_solution(10036627752902092718)
XLA Ops:
  0.6 46.1 %shard_map.68 = (f32[1,2,2,32,128]{4,3,2,1,0:T(8,128)S(1)}, f32[1,2,128,128]{3,2,1,0:T(8,128)S(1)}) custom-call(f32[1,2,2,128,128]{4,3,2,1,0:T(8,128)} %tiles.1, f32[1,2,128,128]{3,2,1,0:T(8,128)} %probe.1, f32[128,128]{1,0:T(8,128)} %phase.1, s32[2,4]{1,0:T(2,128)} %bitcast.1, f32[4,128,128]{2,1,0:T(8,128)} %measured.1), custom_call_target="tpu_custom_call" | custom-call | tf_op jit(solution)/shard_map/pallas_call | solution.py:409
  46.8 0.6 %copy.9 = f32[1,2,2,32,128]{4,3,2,1,0:T(8,128)} copy(f32[1,2,2,32,128]{4,3,2,1,0:T(8,128)S(1)} %get-tuple-element.4) | data formatting | bytes 131072
  47.4 0.7 %copy.10 = f32[1,2,128,128]{3,2,1,0:T(8,128)} copy(f32[1,2,128,128]{3,2,1,0:T(8,128)S(1)} %get-tuple-element.5) | data formatting | bytes 262144
